TPU v7x, 32 devices: a whole 2x2x4 slice. The times are simulated.
32 devices in a mesh: ctx: 16 (over z, x, core), head: 2 (over y).
Axes of the slice: x: 2, y: 2, z: 4, core: 2. Of those that a mesh axis runs over, the one named last changes fastest.
Arguments:
- queries: float32 [16384, 2048], P('ctx', 'head'), may hold values from -5 to 5
- keys: float32 [16384, 2048], P('ctx', 'head'), may hold values from -5 to 5
- values: float32 [16384, 2048], P('ctx', 'head'), may hold values from -6 to 6
- stride_query_w: float32 [2048, 2048], P(None, 'head'), may hold values from -0.53033006 to 0.53033006
- stride_key_w: float32 [2048, 2048], P(None, 'head'), may hold values from -0.53033006 to 0.53033006
- stride_value_w: float32 [2048, 2048], P(None, 'head'), may hold values from -0.70710677 to 0.70710677
- out_weight: float32 [2048, 2048], P('head'), may hold values from -0.5 to 0.5
Outputs:
- mixed: float32 [16384, 2048], P(('ctx', 'head'))
All inputs are finite; a program needn't handle non-finite values.
Results may differ from a plain program's by a relative error of at most 0.0003.
Values sent between devices are 32-bit elements; how exact they have to be, the bound alone decides.
A program may use at most 256 MiB of HBM per device.

v0:
```python
import jax
import jax.numpy as jnp
from jax import lax
from jax.sharding import PartitionSpec as P

HSZ = 128
BAND = 512
STRIDE = 512


def passed_along(block, axis, distance):
    devices = range(lax.axis_size(axis))
    route = [(i - distance, i) for i in devices if i - distance in devices]
    return lax.ppermute(block, axis, route)


def band_block(q_rows, k_rows, v_rows, q_first, k_first):
    scores = jnp.einsum("qhd,khd->hqk", q_rows, k_rows, precision=lax.Precision.HIGHEST) * HSZ ** (
        -0.5
    )
    q_pos = q_first + jnp.arange(q_rows.shape[0], dtype=jnp.int32)[:, None]
    k_pos = k_first + jnp.arange(k_rows.shape[0], dtype=jnp.int32)[None, :]
    allowed = (k_pos <= q_pos) & (k_pos > q_pos - BAND) & (k_pos >= 0)
    scores = jnp.where(allowed[None], scores, -jnp.inf)
    top = jnp.max(scores, axis=-1, keepdims=True)
    weights = jnp.exp(scores - top)
    total = jnp.sum(weights, axis=-1)
    summed = jnp.einsum("hqk,khd->qhd", weights, v_rows, precision=lax.Precision.HIGHEST)
    return summed / jnp.transpose(total)[:, :, None]


def strided_one(q_two, k_two, v_two):
    scores = jnp.einsum("brd,crd->rbc", q_two, k_two, precision=lax.Precision.HIGHEST) * HSZ ** (
        -0.5
    )
    count = q_two.shape[0]
    allowed = (
        jnp.arange(count, dtype=jnp.int32)[None, :] <= jnp.arange(count, dtype=jnp.int32)[:, None]
    )
    scores = jnp.where(allowed[None], scores, -jnp.inf)
    top = jnp.max(scores, axis=-1, keepdims=True)
    weights = jnp.exp(scores - top)
    total = jnp.sum(weights, axis=-1)
    summed = jnp.einsum("rbc,crd->brd", weights, v_two, precision=lax.Precision.HIGHEST)
    return summed / jnp.transpose(total)[:, :, None]


def matmul(left, right):
    return jnp.dot(left, right, precision=lax.Precision.HIGHEST, preferred_element_type=jnp.float32)


def local(queries, keys, values, stride_query_w, stride_key_w, stride_value_w, out_weight):
    rows, width = queries.shape
    heads_here = width // HSZ
    first = lax.axis_index("ctx") * rows
    tails = jnp.stack([keys[rows - BAND :], values[rows - BAND :]])
    before = passed_along(tails, "ctx", 1)
    key_ext = jnp.concatenate([before[0], keys], axis=0).reshape(rows + BAND, heads_here, HSZ)
    value_ext = jnp.concatenate([before[1], values], axis=0).reshape(rows + BAND, heads_here, HSZ)
    q_heads = queries.reshape(rows, heads_here, HSZ)

    def one_block(index):
        offset = index * BAND
        q_rows = lax.dynamic_slice_in_dim(q_heads, offset, BAND, 0)
        k_rows = lax.dynamic_slice_in_dim(key_ext, offset, 2 * BAND, 0)
        v_rows = lax.dynamic_slice_in_dim(value_ext, offset, 2 * BAND, 0)
        return band_block(q_rows, k_rows, v_rows, first + offset, first + offset - BAND)

    banded = lax.map(one_block, jnp.arange(rows // BAND, dtype=jnp.int32)).reshape(rows, width)
    rows_q, rows_k, rows_v = (
        lax.all_to_all(stride_query_w, "head", split_axis=0, concat_axis=1, tiled=True),
        lax.all_to_all(stride_key_w, "head", split_axis=0, concat_axis=1, tiled=True),
        lax.all_to_all(stride_value_w, "head", split_axis=0, concat_axis=1, tiled=True),
    )
    partial_value = jnp.stack(
        [matmul(banded, rows_q), matmul(banded, rows_k), matmul(banded, rows_v)], axis=1
    )
    summed = lax.psum_scatter(partial_value, "head", scatter_dimension=2, tiled=True)
    q_flat, k_flat, v_flat = (summed[:, 0], summed[:, 1], summed[:, 2])
    shape_grouped = (rows // STRIDE, STRIDE, heads_here, HSZ)
    q_two = q_flat.reshape(shape_grouped)
    k_two = k_flat.reshape(shape_grouped)
    v_two = v_flat.reshape(shape_grouped)
    q_two, k_two, v_two = (
        lax.all_to_all(q_two, "ctx", split_axis=1, concat_axis=0, tiled=True),
        lax.all_to_all(k_two, "ctx", split_axis=1, concat_axis=0, tiled=True),
        lax.all_to_all(v_two, "ctx", split_axis=1, concat_axis=0, tiled=True),
    )
    attended = jax.vmap(strided_one, in_axes=2, out_axes=2)(q_two, k_two, v_two)
    restored = lax.all_to_all(attended, "ctx", split_axis=0, concat_axis=1, tiled=True).reshape(
        rows, width
    )
    return lax.psum_scatter(matmul(restored, out_weight), "head", scatter_dimension=0, tiled=True)


def solution(mesh):
    return jax.shard_map(
        local,
        mesh=mesh,
        in_specs=(
            P("ctx", "head"),
            P("ctx", "head"),
            P("ctx", "head"),
            P(None, "head"),
            P(None, "head"),
            P(None, "head"),
            P("head", None),
        ),
        out_specs=P(("ctx", "head"), None),
        check_vma=False,
    )
```

profile of v0, /device:TPU:1, one launch (start us, length us, event | category | flops | bytes accessed | tf_op | source)
XLA Modules:
  0.0 1307.0 jit_solution(18253824402059024621)
XLA Ops:
  6.5 6.9 all-to-all-start.1
  13.5 5.4 copy.43
  18.9 5.3 copy.44
  24.2 2.7 slice_bitcast_fusion.3
  26.9 2.4 pad_maximum_fusion.3
  29.3 4.5 collective-permute-start
  33.8 72.4 %all-to-all-done.1 = f32[2,1024,1024]{2,1,0:T(8,128)} async-done(((f32[2,1024,1024]{2,1,0:T(8,128)}), f32[2,1024,1024]{2,1,0:T(8,128)}, u32[]{:S(2)}, u32[]{:S(2)}) %all-to-all-start.1) | async-done | bytes 8388640 | tf_op jit(solution)/shard_map/all_to_all | solution.py:72
  106.2 7.0 all-to-all-start
  113.2 5.4 copy.46
  118.6 2.8 fusion.36
  122.0 3.5 pad_maximum_fusion.2
  125.9 3.3 pad_maximum_fusion.1
  129.1 75.2 %all-to-all-done = f32[2,1024,1024]{2,1,0:T(8,128)} async-done(((f32[2,1024,1024]{2,1,0:T(8,128)}), f32[2,1024,1024]{2,1,0:T(8,128)}, u32[]{:S(2)}, u32[]{:S(2)}) %all-to-all-start) | async-done | bytes 8388640 | tf_op jit(solution)/shard_map/all_to_all | solution.py:71
  204.3 7.1 all-to-all-start.2
  211.4 109.8 %while.13 = (s32[]{:T(128)}, f32[2,512,8,128]{3,2,1,0:T(8,128)}, s32[2]{0:T(128)S(1)}, f32[1536,8,128]{0,2,1:T(8,128)}, s32[]{:T(128)}, /*index=5*/f32[1024,8,12...) while((s32[]{:T(128)}, f32[2,512,8,128]{3,2,1,0:T(8,128)}, ...), condition=%wide.region_3.4_spmd, body=%wide.region_0.3_spmd.sunk | while | flops 12929462272 | bytes 140610352 | solution.py:69
  213.6 17.7 %fusion.49 = (f32[8,512]{1,0:T(8,128)S(1)}, f32[8,512,1024]{2,1,0:T(8,128)S(1)}) fusion(pred[512,1024]{1,0:T(8,128)(4,1)S(1)} %and_and_fusion.2, f32[1536,8,128]{0,2,1:T(8,128)} %get-tuple-element.246, s32[]{:T(128)S(6)} %select_n.56, f32[1024,8,128]{0,2,1:T(8,128)} %get-tuple-element.245, s32[]{:T(128)S(6)} %select_n.57), kind=kOutput, calls=%fused_computation.2.clone.1 | convolution fusion | flops 6455029760 | bytes 23609352 | tf_op jit(solution)/shard_map/while/body/eval_jaxpr/qhd,khd->hqk/dot_general | solution.py:18
  231.3 4.2 fusion.50
  237.1 25.6 %fusion.51 = f32[1,512,8,128]{1,3,2,0:T(8,128)} fusion(f32[8,512,1024]{2,1,0:T(8,128)} %copy-done, f32[8,512]{1,0:T(8,128)S(1)} %get-tuple-element.213, pred[512,1024]{1,0:T(8,128)(4,1)S(1)} %and_and_fusion.2, f32[1536,8,128]{0,2,1:T(8,128)} %get-tuple-element.243, s32[]{:T(128)S(6)} %select_n.56, f32[512,8]{0,1:T(8,128)S(1)} %bitcast.115), kind=kOutput, calls=%fused_computation.13.clone.1 | convolution fusion | flops 6455558144 | bytes 23625732 | tf_op jit(solution)/shard_map/while/body/eval_jaxpr/hqk,khd->qhd/dot_general | solution.py:28
  268.2 17.7 %fusion.49 = (f32[8,512]{1,0:T(8,128)S(1)}, f32[8,512,1024]{2,1,0:T(8,128)S(1)}) fusion(pred[512,1024]{1,0:T(8,128)(4,1)S(1)} %and_and_fusion.2, f32[1536,8,128]{0,2,1:T(8,128)} %get-tuple-element.246, s32[]{:T(128)S(6)} %select_n.56, f32[1024,8,128]{0,2,1:T(8,128)} %get-tuple-element.245, s32[]{:T(128)S(6)} %select_n.57), kind=kOutput, calls=%fused_computation.2.clone.1 | convolution fusion | flops 6455029760 | bytes 23609352 | tf_op jit(solution)/shard_map/while/body/eval_jaxpr/qhd,khd->hqk/dot_general | solution.py:18
  285.9 4.2 fusion.50
  291.6 25.6 %fusion.51 = f32[1,512,8,128]{1,3,2,0:T(8,128)} fusion(f32[8,512,1024]{2,1,0:T(8,128)} %copy-done, f32[8,512]{1,0:T(8,128)S(1)} %get-tuple-element.213, pred[512,1024]{1,0:T(8,128)(4,1)S(1)} %and_and_fusion.2, f32[1536,8,128]{0,2,1:T(8,128)} %get-tuple-element.243, s32[]{:T(128)S(6)} %select_n.56, f32[512,8]{0,1:T(8,128)S(1)} %bitcast.115), kind=kOutput, calls=%fused_computation.13.clone.1 | convolution fusion | flops 6455558144 | bytes 23625732 | tf_op jit(solution)/shard_map/while/body/eval_jaxpr/hqk,khd->qhd/dot_general | solution.py:28
  321.2 8.8 copy.52
  330.0 8.7 copy.51
  338.6 32.3 %convolution_bitcast_fusion.1 = f32[1024,1,2048]{2,0,1:T(8,128)} fusion(f32[1024,2048]{0,1:T(8,128)} %bitcast.108, f32[128,8,8,128]{3,2,1,0:T(8,128)} %bitcast.119), kind=kOutput, calls=%fused_computation.29 | convolution fusion | flops 25769803776 | bytes 20971520 | tf_op jit(solution)/shard_map/dot_general | solution.py:49
  371.0 31.4 %convolution_bitcast_fusion.2 = f32[1024,1,2048]{2,0,1:T(8,128)} fusion(f32[1024,2048]{0,1:T(8,128)S(1)} %bitcast.109, f32[128,8,8,128]{3,2,1,0:T(8,128)S(1)} %bitcast.121), kind=kOutput, calls=%fused_computation.30 | convolution fusion | flops 25769803776 | bytes 20971520 | tf_op jit(solution)/shard_map/dot_general | solution.py:49
  402.4 8.7 copy.53
  411.0 31.1 %convolution_bitcast_fusion = f32[1024,1,2048]{2,0,1:T(8,128)S(1)} fusion(f32[1024,2048]{0,1:T(8,128)} %bitcast.110, f32[128,8,8,128]{3,2,1,0:T(8,128)} %bitcast.120), kind=kOutput, calls=%fused_computation.28 | convolution fusion | flops 25769803776 | bytes 20971520 | tf_op jit(solution)/shard_map/dot_general | solution.py:49
  442.1 12.6 pad_maximum_fusion
  454.7 282.4 %reduce-scatter.3.cloned.1.call-done = f32[1024,3,1024]{2,0,1:T(8,128)} async-done(((f32[1024,3,2048]{2,0,1:T(8,128)}), f32[1024,3,1024]{2,0,1:T(8,128)}) %reduce-scatter.3.cloned.1.call-update) | async-done | bytes 12582928 | tf_op jit(solution)/shard_map/reduce_scatter | solution.py:78
  737.2 10.3 slice_bitcast_fusion.2
  750.8 6.2 all-to-all-start.4
  757.0 3.2 copy.72
  762.5 72.6 %all-to-all-done.4 = f32[2,512,8,128]{3,2,0,1:T(8,128)} async-done(((f32[2,512,8,128]{3,2,0,1:T(8,128)}), f32[2,512,8,128]{3,2,0,1:T(8,128)}, u32[]{:S(2)}, u32[]{:S(2)}) %all-to-all-start.4) | async-done | bytes 4194336 | tf_op jit(solution)/shard_map/all_to_all | solution.py:85
  835.1 19.3 %all-to-all-start.5 = ((f32[2,512,8,128]{3,2,0,1:T(8,128)}), f32[2,512,8,128]{3,2,0,1:T(8,128)}, u32[]{:S(2)}, u32[]{:S(2)}) async-start(f32[2,512,8,128]{3,2,0,1:T(8,128)} %copy.58), calls=%async_computation.6 | async-start | bytes 8388608 | tf_op jit(solution)/shard_map/all_to_all | solution.py:86
  854.4 3.2 copy.70
  859.9 72.6 %all-to-all-done.5 = f32[2,512,8,128]{3,2,0,1:T(8,128)} async-done(((f32[2,512,8,128]{3,2,0,1:T(8,128)}), f32[2,512,8,128]{3,2,0,1:T(8,128)}, u32[]{:S(2)}, u32[]{:S(2)}) %all-to-all-start.5) | async-done | bytes 4194336 | tf_op jit(solution)/shard_map/all_to_all | solution.py:86
  932.5 19.3 %all-to-all-start.3 = ((f32[2,512,8,128]{3,2,0,1:T(8,128)}), f32[2,512,8,128]{3,2,0,1:T(8,128)}, u32[]{:S(2)}, u32[]{:S(2)}) async-start(f32[2,512,8,128]{3,2,0,1:T(8,128)} %copy.54), calls=%async_computation.4 | async-start | bytes 8388608 | tf_op jit(solution)/shard_map/all_to_all | solution.py:87
  952.2 6.4 copy.57
  958.6 6.3 copy.59
  964.9 64.9 %all-to-all-done.3 = f32[2,512,8,128]{3,2,0,1:T(8,128)} async-done(((f32[2,512,8,128]{3,2,0,1:T(8,128)}), f32[2,512,8,128]{3,2,0,1:T(8,128)}, u32[]{:S(2)}, u32[]{:S(2)}) %all-to-all-start.3) | async-done | bytes 4194336 | tf_op jit(solution)/shard_map/all_to_all | solution.py:87
  1029.8 4.5 copy.55
  1034.6 7.4 fusion.24
  1043.5 8.4 bitcast_divide_fusion.1
  1051.9 2.6 copy.61
  1054.5 112.0 %all_to_all.126 = f32[32,32,8,128]{3,1,2,0:T(8,128)S(1)} all-to-all(f32[32,32,8,128]{3,1,2,0:T(8,128)S(1)} %copy.61), channel_id=1, replica_groups=mesh['ctx'=16,'head'=2] {'ctx'}, dimensions={0} | all-to-all | bytes 8388608 | tf_op jit(solution)/shard_map/all_to_all | solution.py:90
  1166.5 3.8 copy.62
  1170.4 31.3 %fusion.18 = f32[1024,2048]{1,0:T(8,128)} fusion(f32[1024,2048]{1,0:T(8,128)S(1)} %bitcast.118, f32[128,8,8,128]{3,2,1,0:T(8,128)S(1)} %bitcast.114), kind=kOutput, calls=%fused_computation.31 | convolution fusion | flops 25769803776 | bytes 20971520 | tf_op jit(solution)/shard_map/dot_general | solution.py:49
  1201.7 98.1 %reduce-scatter.5.cloned.1.call-done = f32[512,2048]{1,0:T(8,128)} async-done(((f32[1024,2048]{1,0:T(8,128)}), f32[512,2048]{1,0:T(8,128)}) %reduce-scatter.5.cloned.1.call-update) | async-done | bytes 4194320 | tf_op jit(solution)/shard_map/reduce_scatter | solution.py:93
  (51 shorter events, 23.7 us)
Async XLA Ops:
  6.5 99.6 %all-to-all-start.1 = ((f32[2,1024,1024]{2,1,0:T(8,128)}), f32[2,1024,1024]{2,1,0:T(8,128)}, u32[]{:S(2)}, u32[]{:S(2)}) async-start(f32[2,1024,1024]{2,1,0:T(8,128)} %bitcast.105), calls=%async_computation.1 | async-start | bytes 16777216 | tf_op jit(solution)/shard_map/all_to_all | solution.py:72
  29.3 89.3 %collective-permute-start = (f32[2,512,1024]{1,2,0:T(8,128)}, f32[2,512,1024]{1,2,0:T(8,128)}, u32[]{:S(2)}, u32[]{:S(2)}) collective-permute-start(f32[2,512,1024]{1,2,0:T(8,128)} %pad_maximum_fusion.3), channel_id=1, source_target_pairs={{0,2},{2,4},{4,6},{6,8},{8,10},{10,12},{12,14},{14,16},{16,18},{18... | collective-permute-start | bytes 12582920 | tf_op jit(solution)/shard_map/ppermute | solution.py:14
  106.2 98.1 %all-to-all-start = ((f32[2,1024,1024]{2,1,0:T(8,128)}), f32[2,1024,1024]{2,1,0:T(8,128)}, u32[]{:S(2)}, u32[]{:S(2)}) async-start(f32[2,1024,1024]{2,1,0:T(8,128)} %bitcast.106), calls=%async_computation | async-start | bytes 16777216 | tf_op jit(solution)/shard_map/all_to_all | solution.py:71
  118.6 3.4 copy-start.2
  122.0 3.8 copy-start.1
  204.3 198.1 %all-to-all-start.2 = ((f32[2,1024,1024]{2,1,0:T(8,128)}), f32[2,1024,1024]{2,1,0:T(8,128)}, u32[]{:S(2)}, u32[]{:S(2)}) async-start(f32[2,1024,1024]{2,1,0:T(8,128)} %bitcast.107), calls=%async_computation.2 | async-start | bytes 16777216 | tf_op jit(solution)/shard_map/all_to_all | solution.py:73
  211.4 525.8 %reduce-scatter.3.cloned.1.call-start = ((), (), s32[]{:S(2)}) async-start(), calls=%async_computation.9 | async-start | bytes 37748736 | tf_op jit(solution)/shard_map/reduce_scatter | solution.py:78
  231.3 5.7 copy-start
  285.9 5.7 copy-start
  338.6 32.3 %copy-start.5 = (f32[1024,2,1024]{0,2,1:T(8,128)S(1)}, f32[1024,2,1024]{0,2,1:T(8,128)}, u32[]{:S(2)}) copy-start(f32[1024,2,1024]{0,2,1:T(8,128)} %copy.51) | copy-start | bytes 25165828
  338.6 32.3 %copy-start.7 = (f32[2,512,8,128]{3,2,1,0:T(8,128)S(1)}, f32[2,512,8,128]{3,2,1,0:T(8,128)}, u32[]{:S(2)}) copy-start(f32[2,512,8,128]{3,2,1,0:T(8,128)} %get-tuple-element.114) | copy-start | bytes 12582916
  411.0 31.1 %copy-start.6 = (f32[1024,1,2048]{2,0,1:T(8,128)S(1)}, f32[1024,1,2048]{2,0,1:T(8,128)}, u32[]{:S(2)}) copy-start(f32[1024,1,2048]{2,0,1:T(8,128)} %convolution_bitcast_fusion.2) | copy-start | bytes 25165828
  750.8 84.3 %all-to-all-start.4 = ((f32[2,512,8,128]{3,2,0,1:T(8,128)}), f32[2,512,8,128]{3,2,0,1:T(8,128)}, u32[]{:S(2)}, u32[]{:S(2)}) async-start(f32[2,512,8,128]{3,2,0,1:T(8,128)} %copy.56), calls=%async_computation.5 | async-start | bytes 8388608 | tf_op jit(solution)/shard_map/all_to_all | solution.py:85
  835.1 97.4 %all-to-all-start.5 = ((f32[2,512,8,128]{3,2,0,1:T(8,128)}), f32[2,512,8,128]{3,2,0,1:T(8,128)}, u32[]{:S(2)}, u32[]{:S(2)}) async-start(f32[2,512,8,128]{3,2,0,1:T(8,128)} %copy.58), calls=%async_computation.6 | async-start | bytes 8388608 | tf_op jit(solution)/shard_map/all_to_all | solution.py:86
  932.5 97.4 %all-to-all-start.3 = ((f32[2,512,8,128]{3,2,0,1:T(8,128)}), f32[2,512,8,128]{3,2,0,1:T(8,128)}, u32[]{:S(2)}, u32[]{:S(2)}) async-start(f32[2,512,8,128]{3,2,0,1:T(8,128)} %copy.54), calls=%async_computation.4 | async-start | bytes 8388608 | tf_op jit(solution)/shard_map/all_to_all | solution.py:87
  951.8 348.1 %reduce-scatter.5.cloned.1.call-start = ((), (), s32[]{:S(2)}) async-start(), calls=%async_computation.10 | async-start | bytes 12582912 | tf_op jit(solution)/shard_map/reduce_scatter | solution.py:93
  1029.8 4.5 copy-start.3
  1029.8 4.7 copy-start.4
  1054.5 115.8 %slice-start = ((s8[8388608]{0:T(1024)(128)(4,1)}), s8[4194304]{0:T(1024)(128)(4,1)S(1)}, s32[]{:S(2)}) async-start(s8[8388608]{0:T(1024)(128)(4,1)} %bitcast.117), calls=%async_computation.11 | async-start | bytes 8388608
  1166.5 3.9 slice-start.1
Sparse Core Ops, SparseCore 0:
  454.9 282.2 reduce-scatter.2
  1201.9 97.9 reduce-scatter.4
where the time goes:
time: 1310 us
  waiting for transfers between devices  738 us (56%)
  matrix products  229 us (17%)
  blocking collectives  112 us (9%)
  local copies, waits for them, and re-layouts  109 us (8%)
  starting transfers between devices  70.7 us (5%)
  other arithmetic  32.8 us (3%)
  between operations  13.8 us (1%)
    reduce_scatter x1, waiting for transfers between devices, local(): lax.psum_scatter(partial_value, 'head', scatter_dimension=2, tiled=True)  282 us
    dot_general x4, matrix products, matmul(): jnp.dot(left, right, precision=lax.Precision.HIGHEST, preferred_element_t...  126 us
    all_to_all x1, blocking collectives, local(): lax.all_to_all(attended, 'ctx', split_axis=0, concat_axis=1, tiled=True)  112 us
    reduce_scatter x1, waiting for transfers between devices, local(): lax.psum_scatter(matmul(restored, out_weight), 'head', scatter_dimension=...  98.1 us
    all_to_all x1, waiting for transfers between devices, local(): lax.all_to_all(stride_query_w, 'head', split_axis=0, concat_axis=1, tiled...  75.2 us
    all_to_all x1, waiting for transfers between devices, local(): lax.all_to_all(q_two, 'ctx', split_axis=1, concat_axis=0, tiled=True)  72.6 us
    all_to_all x1, waiting for transfers between devices, local(): lax.all_to_all(k_two, 'ctx', split_axis=1, concat_axis=0, tiled=True)  72.6 us
    all_to_all x1, waiting for transfers between devices, local(): lax.all_to_all(stride_key_w, 'head', split_axis=0, concat_axis=1, tiled=T...  72.4 us
  transfers between devices with their start and end apart: 9, of which 7 were waited for; matrix products, arithmetic and copies ran while one was open for 18% of the time, Pallas kernels for 0%

commit v1 on v0

v1 whole, which is shorter than its diff:
```python
import jax
import jax.numpy as jnp
from jax import lax
from jax.sharding import PartitionSpec as P

HSZ = 128
BAND = 512
STRIDE = 512
HIGHEST = lax.Precision.HIGHEST


def passed_along(block, axis, distance):
    devices = range(lax.axis_size(axis))
    route = [(i - distance, i) for i in devices if i - distance in devices]
    return lax.ppermute(block, axis, route)


def band_block(q_rows, k_rows, v_rows, q_first, k_first):
    scores = jnp.einsum("qhd,khd->hqk", q_rows, k_rows, precision=HIGHEST) * HSZ ** (-0.5)
    q_pos = q_first + jnp.arange(q_rows.shape[0], dtype=jnp.int32)[:, None]
    k_pos = k_first + jnp.arange(k_rows.shape[0], dtype=jnp.int32)[None, :]
    allowed = (k_pos <= q_pos) & (k_pos > q_pos - BAND) & (k_pos >= 0)
    scores = jnp.where(allowed[None], scores, -jnp.inf)
    top = jnp.max(scores, axis=-1, keepdims=True)
    weights = jnp.exp(scores - top)
    total = jnp.sum(weights, axis=-1)
    summed = jnp.einsum("hqk,khd->qhd", weights, v_rows, precision=HIGHEST)
    return summed / jnp.transpose(total)[:, :, None]


def strided_one(q_two, k_two, v_two):
    scores = jnp.einsum("brd,crd->rbc", q_two, k_two, precision=HIGHEST) * HSZ ** (-0.5)
    count = q_two.shape[0]
    allowed = (
        jnp.arange(count, dtype=jnp.int32)[None, :] <= jnp.arange(count, dtype=jnp.int32)[:, None]
    )
    scores = jnp.where(allowed[None], scores, -jnp.inf)
    top = jnp.max(scores, axis=-1, keepdims=True)
    weights = jnp.exp(scores - top)
    total = jnp.sum(weights, axis=-1)
    summed = jnp.einsum("rbc,crd->brd", weights, v_two, precision=HIGHEST)
    return summed / jnp.transpose(total)[:, :, None]


def matmul(left, right):
    return jnp.dot(left, right, precision=HIGHEST, preferred_element_type=jnp.float32)


def local(queries, keys, values, stride_query_w, stride_key_w, stride_value_w, out_weight):
    rows, width = queries.shape
    heads_here = width // HSZ
    along, across = lax.axis_size("ctx"), lax.axis_size("head")
    own_rows = rows // across
    piece = own_rows // along
    first = lax.axis_index("ctx") * rows
    tails = jnp.stack([keys[rows - BAND :], values[rows - BAND :]])
    before = passed_along(tails, "ctx", 1)
    groups = 2 if heads_here % 2 == 0 else 1
    part = width // groups
    by_head = (-1, heads_here // groups, HSZ)
    maps = (stride_query_w, stride_key_w, stride_value_w)
    sums = [0.0, 0.0, 0.0]
    for group in range(groups):
        here = slice(group * part, (group + 1) * part)
        later = [
            band_block(
                queries[at : at + BAND, here].reshape(by_head),
                keys[at - BAND : at + BAND, here].reshape(by_head),
                values[at - BAND : at + BAND, here].reshape(by_head),
                first + at,
                first + at - BAND,
            )
            for at in range(BAND, rows, BAND)
        ]
        start = band_block(
            queries[:BAND, here].reshape(by_head),
            jnp.concatenate([before[0][:, here], keys[:BAND, here]], axis=0).reshape(by_head),
            jnp.concatenate([before[1][:, here], values[:BAND, here]], axis=0).reshape(by_head),
            first,
            first - BAND,
        )
        banded = jnp.concatenate([start] + later, axis=0).reshape(across, along, piece, part)
        banded = jnp.transpose(banded, (1, 0, 2, 3))
        banded = lax.all_to_all(banded, "ctx", split_axis=0, concat_axis=0, tiled=True)
        banded = lax.all_gather(banded.reshape(rows, part), "head", axis=1, tiled=True)
        for at, weight in enumerate(maps):
            met = weight.reshape(across, groups, part, width)[:, group].reshape(-1, width)
            sums[at] = sums[at] + matmul(banded, met)
    grouped = (along * (rows // STRIDE), STRIDE // along, heads_here, HSZ)
    q_two, k_two, v_two = (total.reshape(grouped) for total in sums)
    attended = jax.vmap(strided_one, in_axes=2, out_axes=2)(q_two, k_two, v_two)
    attended = attended.reshape(along, across, piece, width)
    attended = jnp.transpose(attended, (1, 0, 2, 3)).reshape(rows, width)
    columns = out_weight.shape[1] // 2
    halves = []
    for at in range(0, 2 * columns, columns):
        share = matmul(attended, out_weight[:, at : at + columns])
        mixed = lax.psum_scatter(share, "head", scatter_dimension=0, tiled=True)
        mixed = mixed.reshape(along, piece, columns)
        mixed = lax.all_to_all(mixed, "ctx", split_axis=0, concat_axis=0, tiled=True)
        halves.append(mixed.reshape(own_rows, columns))
    return jnp.concatenate(halves, axis=1)


def solution(mesh):
    return jax.shard_map(
        local,
        mesh=mesh,
        in_specs=(
            P("ctx", "head"),
            P("ctx", "head"),
            P("ctx", "head"),
            P(None, "head"),
            P(None, "head"),
            P(None, "head"),
            P("head", None),
        ),
        out_specs=P(("ctx", "head"), None),
        check_vma=False,
    )
```

time: 1310 us -> 623 us (0.48)
  waiting for transfers between devices: 738 us -> 125 us
  starting transfers between devices: 70.7 us -> 15.9 us
    all_to_all x6 -> x2, waiting for transfers between devices: 358 us -> 22.4 us  [the longest x1 22.4 us: local(): lax.all_to_all(banded, 'ctx', split_axis=0, concat_axis=0, tiled=True)]
    reduce_scatter x2, waiting for transfers between devices: 381 us -> 86.9 us  [local(): mixed = lax.psum_scatter(share, 'head', scatter_dimension=0, tiled=True)]
    all_to_all x6 -> x2, starting transfers between devices: 65.8 us -> 11.2 us  [the longest x1 6.2 us: local(): lax.all_to_all(mixed, 'ctx', split_axis=0, concat_axis=0, tiled=True)]
    all_to_all x7 -> x0, local copies, waits for them, and re-layouts: 47.2 us -> none  [the longest x1 8.75 us: local(): lax.all_to_all(stride_key_w, 'head', split_axis=0, concat_axis=1, tiled=T...]
    slice x1 -> x13, local copies, waits for them, and re-layouts: 2.83 us -> 40.4 us  [the longest x3 22.5 us: local(): weight.reshape(across, groups, part, width)[:, group].reshape(-1, width)]
    all_gather x0 -> x2, waiting for transfers between devices: none -> 16.1 us  [local(): lax.all_gather(banded.reshape(rows, part), 'head', axis=1, tiled=True)]
    unnamed x25 -> x65, local copies, waits for them, and re-layouts: 35 us -> 45.9 us
    dot_general x10 -> x18, matrix products: 229 us -> 219 us  [the longest x8 126 us: matmul(): jnp.dot(left, right, precision=HIGHEST, preferred_element_type=jnp.float32)]
  transfers between devices with their start and end apart: 9 -> 7, of which waited for: 7 -> 4; matrix products, arithmetic and copies ran while one was open for 18% -> 26% of each run, Pallas kernels for 0% -> 0%
where the time goes in v1:
time: 623 us; the launch traced here: 617 us
  matrix products  219 us (35%)
  waiting for transfers between devices  125 us (20%)
  blocking collectives  112 us (18%)
  local copies, waits for them, and re-layouts  111 us (18%)
  other arithmetic  20.4 us (3%)
  starting transfers between devices  15.9 us (3%)
  between operations  13.9 us (2%)
    dot_general x8, matrix products, matmul(): jnp.dot(left, right, precision=HIGHEST, preferred_element_type=jnp.float32)  126 us
    reduce_scatter x2, waiting for transfers between devices, local(): mixed = lax.psum_scatter(share, 'head', scatter_dimension=0, tiled=True)  86.9 us
    all_to_all x1, blocking collectives, local(): lax.all_to_all(banded, 'ctx', split_axis=0, concat_axis=0, tiled=True)  58.4 us
    all_to_all x1, blocking collectives, local(): lax.all_to_all(mixed, 'ctx', split_axis=0, concat_axis=0, tiled=True)  53.9 us
    unnamed x65, local copies, waits for them, and re-layouts  45.9 us
    dot_general x4, matrix products, band_block(): jnp.einsum('qhd,khd->hqk', q_rows, k_rows, precision=HIGHEST)  35.1 us
    dot_general x4, matrix products, band_block(): summed = jnp.einsum('hqk,khd->qhd', weights, v_rows, precision=HIGHEST)  34.8 us
    slice x3, local copies, waits for them, and re-layouts, local(): weight.reshape(across, groups, part, width)[:, group].reshape(-1, width)  22.5 us
  transfers between devices with their start and end apart: 7, of which 4 were waited for; matrix products, arithmetic and copies ran while one was open for 26% of the time, Pallas kernels for 0%

profile of v1, /device:TPU:1, one launch (start us, length us, event | category | flops | bytes accessed | tf_op | source)
XLA Modules:
  0.0 617.4 jit_solution(7292599190314649279)
XLA Ops:
  13.3 4.7 pad_maximum_fusion
  18.0 4.5 collective-permute-start
  22.6 3.2 fusion.69
  29.7 2.5 fusion.67
  32.2 2.5 copy.128
  34.7 4.3 fusion.68
  39.0 2.6 copy.129
  41.6 2.5 copy.134
  44.1 2.5 copy.135
  46.6 2.6 copy.130
  57.0 2.9 copy.132
  62.1 9.0 %fusion.74 = f32[4,512,1024]{1,2,0:T(8,128)S(1)} fusion(f32[512,4,128]{0,2,1:T(8,128)} %bitcast.158, f32[1024,4,128]{0,2,1:T(8,128)} %bitcast.143), kind=kOutput, calls=%fused_computation.107 | convolution fusion | flops 3221225472 | bytes 11534336 | tf_op jit(solution)/shard_map/qhd,khd->hqk/dot_general | solution.py:19
  71.1 9.5 %fusion.5 = (f32[4,512]{1,0:T(4,128)S(1)}, f32[4,512]{1,0:T(4,128)S(1)}, f32[4,512,1024]{1,2,0:T(8,128)S(1)}) fusion(pred[512,1024]{0,1:T(8,128)(4,1)S(1)} %and_and_fusion, f32[4,512,1024]{1,2,0:T(8,128)S(1)} %fusion.74, f32[512,4,128]{0,2,1:T(8,128)S(1)} %bitcast.150, f32[1024,4,128]{0,2,1:T(8,128)S(1)} %bitcast.132), kind=kOutput, calls=%fused_computation.13 | convolution fusion | flops 3233804288 | bytes 20463616 | tf_op jit(solution)/shard_map/qhd,khd->hqk/dot_general | solution.py:19
  80.6 3.5 fusion.8
  84.1 6.7 %fusion.51 = f32[512,4,128]{0,2,1:T(8,128)S(1)} fusion(f32[1024,4,128]{0,2,1:T(8,128)S(1)} %bitcast.159, f32[4,512,1024]{1,2,0:T(8,128)S(1)} %fusion.74, f32[4,512]{1,0:T(4,128)S(1)} %get-tuple-element.12, pred[512,1024]{0,1:T(8,128)(4,1)S(1)} %and_and_fusion, f32[512,4]{0,1:T(4,128)S(1)} %bitcast.168), kind=kOutput, calls=%fused_computation.75 | convolution fusion | flops 3227779072 | bytes 12075008 | tf_op jit(solution)/shard_map/hqk,khd->qhd/dot_general | solution.py:27
  90.9 2.7 slice_bitcast_fusion
  96.4 7.2 %fusion.73 = f32[4,1024,512]{2,1,0:T(8,128)S(1)} fusion(f32[1024,4,128]{0,2,1:T(8,128)S(1)} %bitcast.146, f32[512,4,128]{0,2,1:T(8,128)S(1)} %bitcast.157), kind=kOutput, calls=%fused_computation.106 | convolution fusion | flops 3221225472 | bytes 11534336 | tf_op jit(solution)/shard_map/qhd,khd->hqk/dot_general | solution.py:19
  105.2 9.5 %fusion.11 = (f32[4,512]{1,0:T(4,128)S(1)}, f32[4,512]{1,0:T(4,128)S(1)}, f32[4,1024,512]{2,1,0:T(8,128)S(1)}) fusion(pred[512,1024]{0,1:T(8,128)(4,1)S(1)} %and_and_fusion.1, f32[4,1024,512]{2,1,0:T(8,128)S(1)} %fusion.73, f32[1024,4,128]{0,2,1:T(8,128)S(1)} %bitcast.133, f32[512,4,128]{0,2,1:T(8,128)S(1)} %bitcast.149), kind=kOutput, calls=%fused_computation.19 | convolution fusion | flops 3233804288 | bytes 20463616 | tf_op jit(solution)/shard_map/qhd,khd->hqk/dot_general | solution.py:19
  114.7 3.5 fusion.3
  118.2 6.6 %fusion.49 = f32[512,4,128]{0,2,1:T(8,128)S(1)} fusion(f32[1024,4,128]{0,2,1:T(8,128)S(1)} %bitcast.163, f32[4,1024,512]{2,1,0:T(8,128)S(1)} %fusion.73, f32[4,512]{1,0:T(4,128)S(1)} %get-tuple-element.8, pred[512,1024]{0,1:T(8,128)(4,1)S(1)} %and_and_fusion.1, f32[512,4]{0,1:T(4,128)S(1)} %bitcast.169), kind=kOutput, calls=%fused_computation.73 | convolution fusion | flops 3227779072 | bytes 12075008 | tf_op jit(solution)/shard_map/hqk,khd->qhd/dot_general | solution.py:27
  130.4 5.0 all-to-all-start
  135.4 2.6 copy.133
  138.0 3.3 copy.138
  141.3 11.6 %fusion.52 = f32[512,4,128]{0,2,1:T(8,128)} fusion(f32[1024,4,128]{0,2,1:T(8,128)} %bitcast.164, f32[4,512,1024]{1,2,0:T(8,128)} %copy-done.1, f32[4,512]{1,0:T(4,128)S(1)} %get-tuple-element.11, pred[512,1024]{0,1:T(8,128)(4,1)S(1)} %and_and_fusion, f32[512,4]{0,1:T(4,128)S(1)} %bitcast.166), kind=kOutput, calls=%fused_computation.76 | convolution fusion | flops 3227779072 | bytes 12075008 | tf_op jit(solution)/shard_map/hqk,khd->qhd/dot_general | solution.py:27
  154.4 22.4 %all-to-all-done = f32[16,2,32,512]{3,2,1,0:T(8,128)S(1)} async-done(((f32[16,2,32,512]{3,2,1,0:T(8,128)}), f32[16,2,32,512]{3,2,1,0:T(8,128)S(1)}, u32[]{:S(2)}, u32[]{:S(2)}) %all-to-all-start) | async-done | bytes 2097184 | tf_op jit(solution)/shard_map/all_to_all | solution.py:84
  178.2 9.9 %fusion.50 = f32[512,4,128]{0,2,1:T(8,128)S(1)} fusion(f32[1024,4,128]{0,2,1:T(8,128)} %bitcast.161, f32[4,1024,512]{2,1,0:T(8,128)} %copy-done.2, f32[4,512]{1,0:T(4,128)S(1)} %get-tuple-element.7, pred[512,1024]{0,1:T(8,128)(4,1)S(1)} %and_and_fusion.1, f32[512,4]{0,1:T(4,128)S(1)} %bitcast.167), kind=kOutput, calls=%fused_computation.74 | convolution fusion | flops 3227779072 | bytes 12075008 | tf_op jit(solution)/shard_map/hqk,khd->qhd/dot_general | solution.py:27
  192.6 58.4 %all_to_all.20 = f32[16,2,32,512]{3,2,1,0:T(8,128)} all-to-all(f32[16,2,32,512]{3,2,1,0:T(8,128)S(1)} %copy.99), channel_id=1, replica_groups=mesh['ctx'=16,'head'=2] {'ctx'}, dimensions={0} | all-to-all | bytes 4194304 | tf_op jit(solution)/shard_map/all_to_all | solution.py:84
  251.1 9.1 %fusion.63 = (f32[2,1,512,1024]{3,2,1,0:T(8,128)}, f32[2,1,512,1024]{3,2,1,0:T(8,128)}) fusion(f32[2,2,512,1024]{3,2,1,0:T(8,128)} %bitcast.134), kind=kLoop, calls=%fused_computation.96 | loop fusion | bytes 16777216 | tf_op jit(solution)/shard_map/slice | solution.py:87
  260.2 9.1 %fusion.64 = (f32[2,1,512,1024]{3,2,1,0:T(8,128)}, f32[2,1,512,1024]{3,2,1,0:T(8,128)}) fusion(f32[2,2,512,1024]{3,2,1,0:T(8,128)} %bitcast.135), kind=kLoop, calls=%fused_computation.97 | loop fusion | bytes 16777216 | tf_op jit(solution)/shard_map/slice | solution.py:87
  269.4 4.2 fusion.65
  273.6 17.7 %fusion.75 = f32[1024,1024]{1,0:T(8,128)} fusion(f32[1024,1024]{1,0:T(8,128)} %all-gather.3.cloned.1.call-done, f32[1024,1024]{1,0:T(8,128)} %bitcast.156), kind=kOutput, calls=%fused_computation.108 | convolution fusion | flops 12884901888 | bytes 12582912 | tf_op jit(solution)/shard_map/dot_general | solution.py:46
  291.3 16.1 %all-gather.5.cloned.1.call-done = f32[1024,1024]{1,0:T(8,128)} async-done(((f32[1024,512]{1,0:T(8,128)}), f32[1024,1024]{1,0:T(8,128)}) %all-gather.5.cloned.1.call-update) | async-done | bytes 4194320 | tf_op jit(solution)/shard_map/all_gather | solution.py:85
  307.5 18.1 %add_bitcast_fusion.2 = f32[128,8,8,128]{3,1,2,0:T(8,128)S(1)} fusion(f32[1024,1024]{1,0:T(8,128)} %fusion.75, f32[1024,1024]{1,0:T(8,128)} %all-gather.5.cloned.1.call-done, f32[1024,1024]{1,0:T(8,128)} %bitcast.131), kind=kOutput, calls=%fused_computation.36 | convolution fusion | flops 12885950464 | bytes 16777216 | tf_op jit(solution)/shard_map/dot_general | solution.py:46
  329.0 14.2 %fusion.76 = f32[1024,1024]{1,0:T(8,128)S(1)} fusion(f32[1024,1024]{1,0:T(8,128)S(1)} %copy-done.21, f32[1024,1024]{1,0:T(8,128)S(1)} %bitcast.155), kind=kOutput, calls=%fused_computation.109 | convolution fusion | flops 12884901888 | bytes 12582912 | tf_op jit(solution)/shard_map/dot_general | solution.py:46
  343.2 13.8 %add_bitcast_fusion.1 = f32[128,8,8,128]{3,1,2,0:T(8,128)S(1)} fusion(f32[1024,1024]{1,0:T(8,128)S(1)} %fusion.76, f32[1024,1024]{1,0:T(8,128)S(1)} %copy-done, f32[1024,1024]{1,0:T(8,128)S(1)} %bitcast.130), kind=kOutput, calls=%fused_computation.35 | convolution fusion | flops 12885950464 | bytes 16777216 | tf_op jit(solution)/shard_map/dot_general | solution.py:46
  359.2 13.8 %fusion.77 = f32[1024,1024]{1,0:T(8,128)S(1)} fusion(f32[1024,1024]{1,0:T(8,128)S(1)} %copy-done.21, f32[1024,1024]{1,0:T(8,128)S(1)} %bitcast.154), kind=kOutput, calls=%fused_computation.110 | convolution fusion | flops 12884901888 | bytes 12582912 | tf_op jit(solution)/shard_map/dot_general | solution.py:46
  373.0 14.0 %add_bitcast_fusion = f32[128,8,8,128]{3,1,2,0:T(8,128)S(1)} fusion(f32[1024,1024]{1,0:T(8,128)S(1)} %fusion.77, f32[1024,1024]{1,0:T(8,128)S(1)} %copy-done, f32[1024,1024]{1,0:T(8,128)S(1)} %bitcast.129), kind=kOutput, calls=%fused_computation.34 | convolution fusion | flops 12885950464 | bytes 16777216 | tf_op jit(solution)/shard_map/dot_general | solution.py:46
  388.0 12.1 %fusion.37 = (f32[8,32,32]{2,1,0:T(8,128)S(1)}, f32[8,32,32,32]{2,3,1,0:T(8,128)S(1)}) fusion(pred[32,32]{0,1:T(8,128)(4,1)S(1)} %iota_compare_fusion, f32[32,32,8,128]{3,2,1,0:T(8,128)S(1)} %bitcast.127, f32[32,32,8,128]{3,2,1,0:T(8,128)S(1)} %bitcast.126), kind=kOutput, calls=%fused_computation.53 | convolution fusion | flops 403431424 | bytes 9470976 | tf_op jit(solution)/shard_map/vmap(brd,crd->rbc)/dot_general | solution.py:32
  401.8 10.8 %bitcast_divide_fusion = f32[32,32,8,128]{3,0,1,2:T(8,128)S(1)} fusion(f32[32,32,8]{0,1,2:T(8,128)S(1)} %bitcast.165, f32[8,32,32,32]{2,3,1,0:T(8,128)S(1)} %get-tuple-element.40, f32[8,32,32]{2,1,0:T(8,128)S(1)} %get-tuple-element.39, pred[32,32]{0,1:T(8,128)(4,1)S(1)} %iota_compare_fusion, f32[32,32,8,128]{3,2,1,0:T(8,128)S(1)} %bitcast.151), kind=kOutput, calls=%fused_computation.22 | convolution fusion | flops 404488192 | bytes 9503744 | tf_op jit(solution)/shard_map/vmap(rbc,crd->brd)/dot_general | solution.py:41
  412.6 4.7 copy.104
  417.3 4.9 reshape.291
  422.2 2.8 copy.105
  426.9 16.3 %fusion.19 = f32[1024,1024]{1,0:T(8,128)} fusion(f32[1024,1024]{1,0:T(8,128)S(1)} %bitcast.152, f32[1024,2048]{1,0:T(8,128)} %param.13), kind=kOutput, calls=%fused_computation.30 | convolution fusion | flops 12884901888 | bytes 12582912 | tf_op jit(solution)/shard_map/dot_general | solution.py:46
  443.3 17.9 %fusion.17 = f32[1024,1024]{1,0:T(8,128)} fusion(f32[1024,1024]{1,0:T(8,128)} %bitcast.153, f32[1024,2048]{1,0:T(8,128)} %param.13), kind=kOutput, calls=%fused_computation.28 | convolution fusion | flops 12884901888 | bytes 12582912 | tf_op jit(solution)/shard_map/dot_general | solution.py:46
  461.3 36.5 %reduce-scatter.3.cloned.1.call-done = f32[512,1024]{1,0:T(8,128)} async-done(((f32[1024,1024]{1,0:T(8,128)}), f32[512,1024]{1,0:T(8,128)}) %reduce-scatter.3.cloned.1.call-update) | async-done | bytes 2097168 | tf_op jit(solution)/shard_map/reduce_scatter | solution.py:98
  497.7 6.2 %all-to-all-start.2 = ((f32[16,32,1024]{2,1,0:T(8,128)}), f32[16,32,1024]{2,1,0:T(8,128)S(1)}, u32[]{:S(2)}, u32[]{:S(2)}) async-start(f32[16,32,1024]{2,1,0:T(8,128)} %bitcast.160), calls=%async_computation.3 | async-start | bytes 4194304 | tf_op jit(solution)/shard_map/all_to_all | solution.py:100
  503.9 50.4 %reduce-scatter.5.cloned.1.call-done = f32[512,1024]{1,0:T(8,128)} async-done(((f32[1024,1024]{1,0:T(8,128)}), f32[512,1024]{1,0:T(8,128)}) %reduce-scatter.5.cloned.1.call-update) | async-done | bytes 2097168 | tf_op jit(solution)/shard_map/reduce_scatter | solution.py:98
  554.3 53.9 %all_to_all.21 = f32[16,32,1024]{2,1,0:T(8,128)S(1)} all-to-all(f32[16,32,1024]{2,1,0:T(8,128)} %bitcast.162), channel_id=1, replica_groups=mesh['ctx'=16,'head'=2] {'ctx'}, dimensions={0} | all-to-all | bytes 4194304 | tf_op jit(solution)/shard_map/all_to_all | solution.py:100
  (99 shorter events, 50.9 us)
Async XLA Ops:
  6.5 1.6 slice-start
  9.9 1.6 slice-start.1
  18.0 72.8 %collective-permute-start = (f32[2,512,1024]{1,2,0:T(8,128)}, f32[2,512,1024]{1,2,0:T(8,128)}, u32[]{:S(2)}, u32[]{:S(2)}) collective-permute-start(f32[2,512,1024]{1,2,0:T(8,128)} %pad_maximum_fusion), channel_id=1, source_target_pairs={{0,2},{2,4},{4,6},{6,8},{8,10},{10,12},{12,14},{14,16},{16,18},{18... | collective-permute-start | bytes 12582920 | tf_op jit(solution)/shard_map/ppermute | solution.py:15
  22.5 3.3 copy-start.4
  22.6 5.2 copy-start.3
  62.1 9.0 %copy-start.9 = (f32[512,512]{0,1:T(8,128)S(1)}, f32[512,512]{0,1:T(8,128)}, u32[]{:S(2)}) copy-start(f32[512,512]{0,1:T(8,128)} %copy.136) | copy-start | bytes 3145732
  80.6 3.5 copy-start.1
  80.6 3.5 copy-start.19
  93.5 1.7 copy-start.11
  95.2 1.2 copy-start.17
  96.4 7.2 %copy-start.12 = (f32[512,512]{0,1:T(8,128)S(1)}, f32[512,512]{0,1:T(8,128)}, u32[]{:S(2)}) copy-start(f32[512,512]{0,1:T(8,128)} %copy.134) | copy-start | bytes 3145732
  103.6 1.2 copy-start.13
  103.7 1.5 copy-start.8
  114.7 3.5 copy-start.2
  130.4 46.5 %all-to-all-start = ((f32[16,2,32,512]{3,2,1,0:T(8,128)}), f32[16,2,32,512]{3,2,1,0:T(8,128)S(1)}, u32[]{:S(2)}, u32[]{:S(2)}) async-start(f32[16,2,32,512]{3,2,1,0:T(8,128)} %copy.82), calls=%async_computation | async-start | bytes 4194304 | tf_op jit(solution)/shard_map/all_to_all | solution.py:84
  135.4 138.2 %all-gather.3.cloned.1.call-start = ((), (), s32[]{:S(2)}) async-start(), calls=%async_computation.6 | async-start | bytes 6291456 | tf_op jit(solution)/shard_map/all_gather | solution.py:85
  141.3 11.6 %copy-start.14 = (f32[512,512]{0,1:T(8,128)S(1)}, f32[512,512]{0,1:T(8,128)}, u32[]{:S(2)}) copy-start(f32[512,512]{0,1:T(8,128)} %copy.133) | copy-start | bytes 3145732
  141.3 11.6 %copy-start.18 = (f32[512,512]{0,1:T(8,128)S(1)}, f32[512,512]{0,1:T(8,128)}, u32[]{:S(2)}) copy-start(f32[512,512]{0,1:T(8,128)} %get-tuple-element.33) | copy-start | bytes 3145732
  176.8 1.3 copy-start.7
  178.2 129.3 %all-gather.5.cloned.1.call-start = ((), (), s32[]{:S(2)}) async-start(), calls=%async_computation.7 | async-start | bytes 6291456 | tf_op jit(solution)/shard_map/all_gather | solution.py:85
  178.2 9.9 %copy-start.20 = (f32[512,4,128]{0,2,1:T(8,128)S(1)}, f32[512,4,128]{0,2,1:T(8,128)}, u32[]{:S(2)}) copy-start(f32[512,4,128]{0,2,1:T(8,128)} %fusion.52) | copy-start | bytes 3145732
  251.0 246.7 %reduce-scatter.3.cloned.1.call-start = ((), (), s32[]{:S(2)}) async-start(), calls=%async_computation.8 | async-start | bytes 6291456 | tf_op jit(solution)/shard_map/reduce_scatter | solution.py:98
  251.1 18.3 %slice-start.2 = ((s8[8388608]{0:T(1024)(128)(4,1)}), s8[4194304]{0:T(1024)(128)(4,1)S(1)}, s32[]{:S(2)}) async-start(s8[8388608]{0:T(1024)(128)(4,1)} %bitcast.136), calls=%async_computation.12 | async-start | bytes 8388608
  260.2 9.2 %slice-start.3 = ((s8[8388608]{0:T(1024)(128)(4,1)}), s8[4194304]{0:T(1024)(128)(4,1)S(1)}, s32[]{:S(2)}) async-start(s8[8388608]{0:T(1024)(128)(4,1)} %bitcast.136), calls=%async_computation.13 | async-start | bytes 8388608
  325.6 2.2 copy-start.16
  325.6 3.5 copy-start.21
  329.0 14.2 %copy-start = (f32[1024,1024]{1,0:T(8,128)S(1)}, f32[1024,1024]{1,0:T(8,128)}, u32[]{:S(2)}) copy-start(f32[1024,1024]{1,0:T(8,128)} %all-gather.5.cloned.1.call-done) | copy-start | bytes 12582916
  329.0 14.2 %copy-start.6 = (f32[2,1,512,1024]{3,2,1,0:T(8,128)S(1)}, f32[2,1,512,1024]{3,2,1,0:T(8,128)}, u32[]{:S(2)}) copy-start(f32[2,1,512,1024]{3,2,1,0:T(8,128)} %get-tuple-element.15) | copy-start | bytes 12582916
  357.0 2.2 copy-start.15
  359.2 13.8 %copy-start.5 = (f32[2,1,512,1024]{3,2,1,0:T(8,128)S(1)}, f32[2,1,512,1024]{3,2,1,0:T(8,128)}, u32[]{:S(2)}) copy-start(f32[2,1,512,1024]{3,2,1,0:T(8,128)} %get-tuple-element.17) | copy-start | bytes 12582916
  424.9 2.0 copy-start.10
  443.3 111.0 %reduce-scatter.5.cloned.1.call-start = ((), (), s32[]{:S(2)}) async-start(), calls=%async_computation.9 | async-start | bytes 6291456 | tf_op jit(solution)/shard_map/reduce_scatter | solution.py:98
  497.7 56.6 %all-to-all-start.2 = ((f32[16,32,1024]{2,1,0:T(8,128)}), f32[16,32,1024]{2,1,0:T(8,128)S(1)}, u32[]{:S(2)}, u32[]{:S(2)}) async-start(f32[16,32,1024]{2,1,0:T(8,128)} %bitcast.160), calls=%async_computation.3 | async-start | bytes 4194304 | tf_op jit(solution)/shard_map/all_to_all | solution.py:100
Sparse Core Ops, SparseCore 0:
  178.3 62.3 all-gather.2
  251.2 56.2 all-gather.4
  443.4 54.2 reduce-scatter.2
  500.0 54.3 reduce-scatter.4

commit v2 on v1

v2 whole, which is shorter than its diff:
```python
import jax
import jax.numpy as jnp
from jax import lax
from jax.experimental import pallas as pl
from jax.experimental.pallas import tpu as pltpu
from jax.sharding import PartitionSpec as P

HSZ = 128
BAND = 512
STRIDE = 512
HIGHEST = lax.Precision.HIGHEST


def passed_along(block, axis, distance):
    devices = range(lax.axis_size(axis))
    route = [(i - distance, i) for i in devices if i - distance in devices]
    return lax.ppermute(block, axis, route)


def band_kernel(valid_ref, q_ref, k_ref, v_ref, old_k_ref, old_v_ref, out_ref):
    valid = valid_ref[0, 0] > 0
    step = BAND // 2
    across_last = (((1,), (1,)), ((), ()))
    for low in range(0, BAND, step):
        q_rows = q_ref[low : low + step, :]
        old = lax.dot_general(q_rows, old_k_ref[low:, :], across_last, precision=HIGHEST)
        new = lax.dot_general(q_rows, k_ref[: low + step, :], across_last, precision=HIGHEST)
        old_row = lax.broadcasted_iota(jnp.int32, old.shape, 0)
        old_column = lax.broadcasted_iota(jnp.int32, old.shape, 1)
        new_row = lax.broadcasted_iota(jnp.int32, new.shape, 0)
        new_column = lax.broadcasted_iota(jnp.int32, new.shape, 1)
        old = jnp.where((old_column > old_row) & valid, old * HSZ ** (-0.5), -jnp.inf)
        new = jnp.where(new_column <= new_row + low, new * HSZ ** (-0.5), -jnp.inf)
        top = jnp.maximum(
            jnp.max(old, axis=1, keepdims=True), jnp.max(new, axis=1, keepdims=True)
        )
        old, new = jnp.exp(old - top), jnp.exp(new - top)
        total = jnp.sum(old, axis=1, keepdims=True) + jnp.sum(new, axis=1, keepdims=True)
        summed = jnp.dot(
            old, old_v_ref[low:, :], precision=HIGHEST, preferred_element_type=jnp.float32
        ) + jnp.dot(
            new, v_ref[: low + step, :], precision=HIGHEST, preferred_element_type=jnp.float32
        )
        out_ref[low : low + step, :] = summed / total


def band(valid, queries, keys, values, old_k, old_v, first_block, blocks, first_head, heads):
    def own(head, block):
        return first_block + block, first_head + head

    def before(head, block):
        return block, first_head + head

    tile = (BAND, HSZ)
    work = heads * blocks * BAND * BAND * HSZ
    return pl.pallas_call(
        band_kernel,
        grid=(heads, blocks),
        out_shape=jax.ShapeDtypeStruct((blocks * BAND, heads * HSZ), jnp.float32),
        in_specs=[
            pl.BlockSpec(memory_space=pltpu.SMEM),
            pl.BlockSpec(tile, own),
            pl.BlockSpec(tile, own),
            pl.BlockSpec(tile, own),
            pl.BlockSpec(tile, before),
            pl.BlockSpec(tile, before),
        ],
        out_specs=pl.BlockSpec(tile, lambda head, block: (block, head)),
        compiler_params=pltpu.CompilerParams(vmem_limit_bytes=32 * 2**20),
        cost_estimate=pl.CostEstimate(
            flops=36 * work, bytes_accessed=24 * heads * blocks * BAND * HSZ, transcendentals=0
        ),
    )(valid, queries, keys, values, old_k, old_v)


def strided_one(q_two, k_two, v_two):
    scores = jnp.einsum("brd,crd->rbc", q_two, k_two, precision=HIGHEST) * HSZ ** (-0.5)
    count = q_two.shape[0]
    allowed = (
        jnp.arange(count, dtype=jnp.int32)[None, :] <= jnp.arange(count, dtype=jnp.int32)[:, None]
    )
    scores = jnp.where(allowed[None], scores, -jnp.inf)
    top = jnp.max(scores, axis=-1, keepdims=True)
    weights = jnp.exp(scores - top)
    total = jnp.sum(weights, axis=-1)
    summed = jnp.einsum("rbc,crd->brd", weights, v_two, precision=HIGHEST)
    return summed / jnp.transpose(total)[:, :, None]


def matmul(left, right):
    return jnp.dot(left, right, precision=HIGHEST, preferred_element_type=jnp.float32)


def local(queries, keys, values, stride_query_w, stride_key_w, stride_value_w, out_weight):
    rows, width = queries.shape
    heads_here = width // HSZ
    along, across = lax.axis_size("ctx"), lax.axis_size("head")
    own_rows = rows // across
    piece = own_rows // along
    count = rows // BAND
    every = jnp.ones((1, 1), jnp.int32)
    not_first = (lax.axis_index("ctx") > 0).astype(jnp.int32).reshape(1, 1)
    old_k = passed_along(keys[rows - BAND :], "ctx", 1)
    old_v = passed_along(values[rows - BAND :], "ctx", 1)
    groups = 2 if heads_here % 2 == 0 else 1
    part = width // groups
    few = heads_here // groups
    laters = [
        band(every, queries, keys, values, keys, values, 1, count - 1, group * few, few)
        for group in range(groups)
    ]
    maps = (stride_query_w, stride_key_w, stride_value_w)
    sums = [0.0, 0.0, 0.0]
    for group in range(groups):
        start = band(not_first, queries, keys, values, old_k, old_v, 0, 1, group * few, few)
        banded = jnp.concatenate([start, laters[group]], axis=0)
        banded = jnp.transpose(banded.reshape(across, along, piece, part), (1, 0, 2, 3))
        banded = lax.all_to_all(banded, "ctx", split_axis=0, concat_axis=0, tiled=True)
        banded = lax.all_gather(banded.reshape(rows, part), "head", axis=1, tiled=True)
        for at, weight in enumerate(maps):
            met = weight.reshape(across, groups, part, width)[:, group].reshape(-1, width)
            sums[at] = sums[at] + matmul(banded, met)
    grouped = (along * (rows // STRIDE), STRIDE // along, heads_here, HSZ)
    q_two, k_two, v_two = (total.reshape(grouped) for total in sums)
    attended = jax.vmap(strided_one, in_axes=2, out_axes=2)(q_two, k_two, v_two)
    attended = attended.reshape(along, across, piece, width)
    attended = jnp.transpose(attended, (1, 0, 2, 3)).reshape(rows, width)
    columns = out_weight.shape[1] // 4
    quarters = []
    for at in range(0, 4 * columns, columns):
        share = matmul(attended, out_weight[:, at : at + columns])
        mixed = lax.psum_scatter(share, "head", scatter_dimension=0, tiled=True)
        mixed = mixed.reshape(along, piece, columns)
        mixed = lax.all_to_all(mixed, "ctx", split_axis=0, concat_axis=0, tiled=True)
        quarters.append(mixed.reshape(own_rows, columns))
    return jnp.concatenate(quarters, axis=1)


def solution(mesh):
    return jax.shard_map(
        local,
        mesh=mesh,
        in_specs=(
            P("ctx", "head"),
            P("ctx", "head"),
            P("ctx", "head"),
            P(None, "head"),
            P(None, "head"),
            P(None, "head"),
            P("head", None),
        ),
        out_specs=P(("ctx", "head"), None),
        check_vma=False,
    )
```

time: 623 us -> 581 us (0.933)
  Pallas kernels: 0 us -> 69.4 us
  matrix products: 219 us -> 157 us
  local copies, waits for them, and re-layouts: 111 us -> 69.8 us
  blocking collectives: 112 us -> 89.9 us
  starting transfers between devices: 15.9 us -> 32.7 us
  other arithmetic: 20.4 us -> 4.42 us
  waiting for transfers between devices: 125 us -> 137 us
    dot_general x8 -> x0, matrix products: 69.9 us -> none  [the longest x4 35.1 us: band_block(): jnp.einsum('qhd,khd->hqk', q_rows, k_rows, precision=HIGHEST)]
    pallas_call x0 -> x4, Pallas kernels: none -> 69.4 us  [band(): pl.pallas_call(band_kernel, grid=(heads, blocks), out_shape=jax.ShapeDtyp...]
    all_to_all x1, blocking collectives: 53.9 us -> 31.4 us  [local(): lax.all_to_all(mixed, 'ctx', split_axis=0, concat_axis=0, tiled=True)]
    ppermute x1 -> x2, waiting for transfers between devices: 0.01 us -> 18.7 us  [passed_along(): return lax.ppermute(block, axis, route)]
    unnamed x65 -> x45, local copies, waits for them, and re-layouts: 45.9 us -> 28.7 us
    slice x10 -> x2, local copies, waits for them, and re-layouts: 17.9 us -> 4.8 us  [the longest x1 3.34 us: local(): old_v = passed_along(values[rows - BAND:], 'ctx', 1)]
    all_to_all x1 -> x3, starting transfers between devices: 6.2 us -> 18.6 us  [local(): lax.all_to_all(mixed, 'ctx', split_axis=0, concat_axis=0, tiled=True)]
    dot_general x8 -> x10, matrix products: 126 us -> 134 us  [matmul(): jnp.dot(left, right, precision=HIGHEST, preferred_element_type=jnp.float32)]
  transfers between devices with their start and end apart: 7 -> 12, of which waited for: 4 -> 7; matrix products, arithmetic and copies ran while one was open for 26% -> 13% of each run, Pallas kernels for 0% -> 9%
where the time goes in v2:
time: 581 us; the launch traced here: 574 us
  matrix products  157 us (27%)
  waiting for transfers between devices  137 us (24%)
  blocking collectives  89.9 us (15%)
  local copies, waits for them, and re-layouts  69.8 us (12%)
  Pallas kernels  69.4 us (12%)
  starting transfers between devices  32.7 us (6%)
  between operations  14.2 us (2%)
    dot_general x10, matrix products, matmul(): jnp.dot(left, right, precision=HIGHEST, preferred_element_type=jnp.float32)  134 us
    reduce_scatter x4, waiting for transfers between devices, local(): mixed = lax.psum_scatter(share, 'head', scatter_dimension=0, tiled=True)  84.2 us
    pallas_call x4, Pallas kernels, band(): pl.pallas_call(band_kernel, grid=(heads, blocks), out_shape=jax.ShapeDtyp...  69.4 us
    all_to_all x1, blocking collectives, local(): lax.all_to_all(banded, 'ctx', split_axis=0, concat_axis=0, tiled=True)  58.5 us
    all_to_all x1, blocking collectives, local(): lax.all_to_all(mixed, 'ctx', split_axis=0, concat_axis=0, tiled=True)  31.4 us
    unnamed x45, local copies, waits for them, and re-layouts  28.7 us
    slice x3, local copies, waits for them, and re-layouts, local(): weight.reshape(across, groups, part, width)[:, group].reshape(-1, width)  22.5 us
    ppermute x2, waiting for transfers between devices, passed_along(): return lax.ppermute(block, axis, route)  18.7 us
  transfers between devices with their start and end apart: 12, of which 7 were waited for; matrix products, arithmetic and copies ran while one was open for 13% of the time, Pallas kernels for 9%

profile of v2, /device:TPU:1, one launch (start us, length us, event | category | flops | bytes accessed | tf_op | source)
XLA Modules:
  0.0 573.6 jit_solution(15645598053080876661)
XLA Ops:
  6.5 3.3 slice.37
  9.9 4.5 collective-permute-start.1
  17.8 2.2 copy-done.1
  20.0 2.2 copy-done.5
  22.2 2.2 copy-done.9
  24.3 17.0 %shard_map.74 = f32[512,512]{1,0:T(8,128)S(1)} custom-call(s32[1,1]{1,0:T(1,128)} %constant.5.clone.1.valid_ref, f32[1024,1024]{1,0:T(8,128)S(1)} %copy-done.9, f32[1024,1024]{1,0:T(8,128)S(1)} %copy-done.1, f32[1024,1024]{1,0:T(8,128)S(1)} %copy-done.5, f32[1024,1024]{1,0:T(8,128)S(1)} %copy-done.1, f32[1024,1024]{1,0:T(8,128)S(1)} %copy-done.5), custom_call_target="tpu_custom_call" | custom-call | flops 4831838208 | bytes 6291456 | tf_op jit(solution)/shard_map/pallas_call | solution.py:56
  41.4 18.7 %collective-permute-done.old_k_ref = f32[512,1024]{1,0:T(8,128)} collective-permute-done((f32[512,1024]{1,0:T(8,128)}, f32[512,1024]{1,0:T(8,128)}, u32[]{:S(2)}, u32[]{:S(2)}) %collective-permute-start) | collective-permute-done | bytes 2097184 | tf_op jit(solution)/shard_map/ppermute | solution.py:17
  60.1 17.7 %shard_map.73 = f32[512,512]{1,0:T(8,128)S(1)} custom-call(s32[1,1]{1,0:T(1,128)} %bitcast.valid_ref, f32[1024,1024]{1,0:T(8,128)S(1)} %copy-done.9, f32[1024,1024]{1,0:T(8,128)S(1)} %copy-done.2, f32[1024,1024]{1,0:T(8,128)S(1)} %copy-done.6, f32[512,1024]{1,0:T(8,128)} %collective-permute-done.old_k_ref, f32[512,1024]{1,0:T(8,128)S(1)} %collective-permute-done.1.old_v_ref), custom_call_target="tpu_custom_call" | custom-call | flops 4831838208 | bytes 6291456 | tf_op jit(solution)/shard_map/pallas_call | solution.py:56
  79.6 7.2 %all-to-all-start = ((f32[16,2,32,512]{3,2,1,0:T(8,128)}), f32[16,2,32,512]{3,2,1,0:T(8,128)}, u32[]{:S(2)}, u32[]{:S(2)}) async-start(f32[16,2,32,512]{3,2,1,0:T(8,128)} %bitcast.79), calls=%async_computation | async-start | bytes 4194304 | tf_op jit(solution)/shard_map/all_to_all | solution.py:118
  87.0 2.2 copy-done.3
  89.2 2.2 copy-done.7
  91.4 2.2 copy-done.10
  93.6 17.1 %shard_map.76 = f32[512,512]{1,0:T(8,128)S(1)} custom-call(s32[1,1]{1,0:T(1,128)} %constant.5.clone.1.valid_ref, f32[1024,1024]{1,0:T(8,128)S(1)} %copy-done.10, f32[1024,1024]{1,0:T(8,128)S(1)} %copy-done.3, f32[1024,1024]{1,0:T(8,128)S(1)} %copy-done.7, f32[1024,1024]{1,0:T(8,128)S(1)} %copy-done.3, f32[1024,1024]{1,0:T(8,128)S(1)} %copy-done.7), custom_call_target="tpu_custom_call" | custom-call | flops 4831838208 | bytes 6291456 | tf_op jit(solution)/shard_map/pallas_call | solution.py:56
  110.7 17.7 %all-to-all-done = f32[16,2,32,512]{3,2,1,0:T(8,128)} async-done(((f32[16,2,32,512]{3,2,1,0:T(8,128)}), f32[16,2,32,512]{3,2,1,0:T(8,128)}, u32[]{:S(2)}, u32[]{:S(2)}) %all-to-all-start) | async-done | bytes 2097184 | tf_op jit(solution)/shard_map/all_to_all | solution.py:118
  128.4 2.2 copy-done.4
  130.6 2.2 copy-done.8
  132.8 2.2 copy-done.11
  135.0 17.7 %shard_map.75 = f32[512,512]{1,0:T(8,128)S(1)} custom-call(s32[1,1]{1,0:T(1,128)} %bitcast.valid_ref, f32[1024,1024]{1,0:T(8,128)S(1)} %copy-done.11, f32[1024,1024]{1,0:T(8,128)S(1)} %copy-done.4, f32[1024,1024]{1,0:T(8,128)S(1)} %copy-done.8, f32[512,1024]{1,0:T(8,128)} %collective-permute-done.old_k_ref, f32[512,1024]{1,0:T(8,128)S(1)} %collective-permute-done.1.old_v_ref), custom_call_target="tpu_custom_call" | custom-call | flops 4831838208 | bytes 6291456 | tf_op jit(solution)/shard_map/pallas_call | solution.py:56
  153.1 58.5 %all_to_all.30 = f32[16,2,32,512]{3,2,1,0:T(8,128)} all-to-all(f32[16,2,32,512]{3,2,1,0:T(8,128)S(1)} %bitcast.82), channel_id=1, replica_groups=mesh['ctx'=16,'head'=2] {'ctx'}, dimensions={0} | all-to-all | bytes 4194304 | tf_op jit(solution)/shard_map/all_to_all | solution.py:118
  211.7 9.1 %fusion.24 = (f32[2,1,512,1024]{3,2,1,0:T(8,128)}, f32[2,1,512,1024]{3,2,1,0:T(8,128)}) fusion(f32[2,2,512,1024]{3,2,1,0:T(8,128)} %bitcast.73), kind=kLoop, calls=%fused_computation.34 | loop fusion | bytes 16777216 | tf_op jit(solution)/shard_map/slice | solution.py:121
  220.8 9.3 %fusion.25 = (f32[2,1,512,1024]{3,2,1,0:T(8,128)}, f32[2,1,512,1024]{3,2,1,0:T(8,128)}) fusion(f32[2,2,512,1024]{3,2,1,0:T(8,128)} %bitcast.74), kind=kLoop, calls=%fused_computation.35 | loop fusion | bytes 16777216 | tf_op jit(solution)/shard_map/slice | solution.py:121
  230.1 4.1 fusion.23
  234.2 18.0 %fusion.27 = f32[1024,1024]{1,0:T(8,128)} fusion(f32[1024,1024]{1,0:T(8,128)} %all-gather.3.cloned.1.call-done, f32[1024,1024]{1,0:T(8,128)} %bitcast.86), kind=kOutput, calls=%fused_computation.37 | convolution fusion | flops 12884901888 | bytes 12582912 | tf_op jit(solution)/shard_map/dot_general | solution.py:91
  252.2 15.8 %all-gather.5.cloned.1.call-done = f32[1024,1024]{1,0:T(8,128)} async-done(((f32[1024,512]{1,0:T(8,128)}), f32[1024,1024]{1,0:T(8,128)}) %all-gather.5.cloned.1.call-update) | async-done | bytes 4194320 | tf_op jit(solution)/shard_map/all_gather | solution.py:119
  268.0 18.0 %add_bitcast_fusion.1 = f32[128,8,8,128]{3,1,2,0:T(8,128)S(1)} fusion(f32[1024,1024]{1,0:T(8,128)} %fusion.27, f32[1024,1024]{1,0:T(8,128)} %all-gather.5.cloned.1.call-done, f32[1024,1024]{1,0:T(8,128)} %bitcast.72), kind=kOutput, calls=%fused_computation.10 | convolution fusion | flops 12885950464 | bytes 16777216 | tf_op jit(solution)/shard_map/dot_general | solution.py:91
  289.6 14.3 %fusion.28 = f32[1024,1024]{1,0:T(8,128)S(1)} fusion(f32[1024,1024]{1,0:T(8,128)S(1)} %copy-done.18, f32[1024,1024]{1,0:T(8,128)S(1)} %bitcast.85), kind=kOutput, calls=%fused_computation.38 | convolution fusion | flops 12884901888 | bytes 12582912 | tf_op jit(solution)/shard_map/dot_general | solution.py:91
  303.9 13.9 %add_bitcast_fusion = f32[128,8,8,128]{3,1,2,0:T(8,128)S(1)} fusion(f32[1024,1024]{1,0:T(8,128)S(1)} %fusion.28, f32[1024,1024]{1,0:T(8,128)S(1)} %copy-done.13, f32[1024,1024]{1,0:T(8,128)S(1)} %bitcast.71), kind=kOutput, calls=%fused_computation.9 | convolution fusion | flops 12885950464 | bytes 16777216 | tf_op jit(solution)/shard_map/dot_general | solution.py:91
  320.0 15.6 %fusion.26 = f32[1024,1024]{1,0:T(8,128)S(1)} fusion(f32[1024,1024]{1,0:T(8,128)} %all-gather.3.cloned.1.call-done, f32[1024,1024]{1,0:T(8,128)S(1)} %bitcast.84), kind=kOutput, calls=%fused_computation.36 | convolution fusion | flops 12884901888 | bytes 12582912 | tf_op jit(solution)/shard_map/dot_general | solution.py:91
  335.6 13.9 %add_bitcast_fusion.2 = f32[128,8,8,128]{3,1,2,0:T(8,128)S(1)} fusion(f32[1024,1024]{1,0:T(8,128)S(1)} %fusion.26, f32[1024,1024]{1,0:T(8,128)S(1)} %copy-done.13, f32[1024,1024]{1,0:T(8,128)S(1)} %bitcast.70), kind=kOutput, calls=%fused_computation.11 | convolution fusion | flops 12885950464 | bytes 16777216 | tf_op jit(solution)/shard_map/dot_general | solution.py:91
  351.0 11.7 %fusion.5 = (f32[8,32,32]{2,1,0:T(8,128)S(1)}, f32[8,32,32,32]{2,3,1,0:T(8,128)S(1)}) fusion(pred[32,32]{0,1:T(8,128)(4,1)S(1)} %iota_compare_fusion, f32[32,32,8,128]{3,2,1,0:T(8,128)S(1)} %bitcast.68, f32[32,32,8,128]{3,2,1,0:T(8,128)S(1)} %bitcast.67), kind=kOutput, calls=%fused_computation.12 | convolution fusion | flops 403431424 | bytes 9470976 | tf_op jit(solution)/shard_map/vmap(brd,crd->rbc)/dot_general | solution.py:77
  364.4 11.0 %bitcast_divide_fusion = f32[32,32,8,128]{3,0,1,2:T(8,128)S(1)} fusion(f32[32,32,8]{0,1,2:T(8,128)S(1)} %bitcast.95, f32[8,32,32,32]{2,3,1,0:T(8,128)S(1)} %get-tuple-element.12, f32[8,32,32]{2,1,0:T(8,128)S(1)} %get-tuple-element.11, pred[32,32]{0,1:T(8,128)(4,1)S(1)} %iota_compare_fusion, f32[32,32,8,128]{3,2,1,0:T(8,128)S(1)} %bitcast.83), kind=kOutput, calls=%fused_computation.1 | convolution fusion | flops 404488192 | bytes 9503744 | tf_op jit(solution)/shard_map/vmap(rbc,crd->brd)/dot_general | solution.py:86
  375.5 4.4 copy.18
  379.9 4.9 reshape.82
  384.8 2.5 copy.19
  387.3 2.0 copy-done.12
  389.3 9.2 %fusion.7 = f32[1024,512]{1,0:T(8,128)} fusion(f32[1024,1024]{1,0:T(8,128)S(1)} %bitcast.63, f32[1024,2048]{1,0:T(8,128)} %param.13), kind=kOutput, calls=%fused_computation.18 | convolution fusion | flops 6442450944 | bytes 8388608 | tf_op jit(solution)/shard_map/dot_general | solution.py:91
  398.6 10.2 %fusion.9 = f32[1024,512]{1,0:T(8,128)} fusion(f32[1024,1024]{1,0:T(8,128)} %bitcast.64, f32[1024,2048]{1,0:T(8,128)} %param.13), kind=kOutput, calls=%fused_computation.20 | convolution fusion | flops 6442450944 | bytes 8388608 | tf_op jit(solution)/shard_map/dot_general | solution.py:91
  408.9 10.5 %fusion.11 = f32[1024,512]{1,0:T(8,128)} fusion(f32[1024,1024]{1,0:T(8,128)} %bitcast.65, f32[1024,2048]{1,0:T(8,128)} %param.13), kind=kOutput, calls=%fused_computation.22 | convolution fusion | flops 6442450944 | bytes 8388608 | tf_op jit(solution)/shard_map/dot_general | solution.py:91
  419.4 11.1 %reduce-scatter.11.cloned.1.call-done = f32[512,512]{1,0:T(8,128)} async-done(((f32[1024,512]{1,0:T(8,128)}), f32[512,512]{1,0:T(8,128)}) %reduce-scatter.11.cloned.1.call-update) | async-done | bytes 1048592 | tf_op jit(solution)/shard_map/reduce_scatter | solution.py:132
  430.5 6.2 %all-to-all-start.5 = ((f32[16,32,512]{2,1,0:T(8,128)}), f32[16,32,512]{2,1,0:T(8,128)S(1)}, u32[]{:S(2)}, u32[]{:S(2)}) async-start(f32[16,32,512]{2,1,0:T(8,128)} %bitcast.93), calls=%async_computation.9 | async-start | bytes 2097152 | tf_op jit(solution)/shard_map/all_to_all | solution.py:134
  436.7 10.3 %fusion.13 = f32[1024,512]{1,0:T(8,128)} fusion(f32[1024,1024]{1,0:T(8,128)} %bitcast.66, f32[1024,2048]{1,0:T(8,128)} %param.13), kind=kOutput, calls=%fused_computation.24 | convolution fusion | flops 6442450944 | bytes 8388608 | tf_op jit(solution)/shard_map/dot_general | solution.py:91
  447.0 17.5 %reduce-scatter.9.cloned.1.call-done = f32[512,512]{1,0:T(8,128)} async-done(((f32[1024,512]{1,0:T(8,128)}), f32[512,512]{1,0:T(8,128)}) %reduce-scatter.9.cloned.1.call-update) | async-done | bytes 1048592 | tf_op jit(solution)/shard_map/reduce_scatter | solution.py:132
  464.6 6.2 %all-to-all-start.4 = ((f32[16,32,512]{2,1,0:T(8,128)}), f32[16,32,512]{2,1,0:T(8,128)S(1)}, u32[]{:S(2)}, u32[]{:S(2)}) async-start(f32[16,32,512]{2,1,0:T(8,128)} %bitcast.92), calls=%async_computation.7 | async-start | bytes 2097152 | tf_op jit(solution)/shard_map/all_to_all | solution.py:134
  470.8 27.7 %reduce-scatter.7.cloned.1.call-done = f32[512,512]{1,0:T(8,128)} async-done(((f32[1024,512]{1,0:T(8,128)}), f32[512,512]{1,0:T(8,128)}) %reduce-scatter.7.cloned.1.call-update) | async-done | bytes 1048592 | tf_op jit(solution)/shard_map/reduce_scatter | solution.py:132
  498.5 6.2 %all-to-all-start.3 = ((f32[16,32,512]{2,1,0:T(8,128)}), f32[16,32,512]{2,1,0:T(8,128)S(1)}, u32[]{:S(2)}, u32[]{:S(2)}) async-start(f32[16,32,512]{2,1,0:T(8,128)} %bitcast.91), calls=%async_computation.5 | async-start | bytes 2097152 | tf_op jit(solution)/shard_map/all_to_all | solution.py:134
  504.7 27.9 %reduce-scatter.5.cloned.1.call-done = f32[512,512]{1,0:T(8,128)} async-done(((f32[1024,512]{1,0:T(8,128)}), f32[512,512]{1,0:T(8,128)}) %reduce-scatter.5.cloned.1.call-update) | async-done | bytes 1048592 | tf_op jit(solution)/shard_map/reduce_scatter | solution.py:132
  532.6 31.4 %all_to_all.31 = f32[16,32,512]{2,1,0:T(8,128)S(1)} all-to-all(f32[16,32,512]{2,1,0:T(8,128)} %bitcast.94), channel_id=1, replica_groups=mesh['ctx'=16,'head'=2] {'ctx'}, dimensions={0} | all-to-all | bytes 2097152 | tf_op jit(solution)/shard_map/all_to_all | solution.py:134
  564.0 2.4 pad_maximum_fusion
  (61 shorter events, 14.9 us)
Async XLA Ops:
  6.5 7.9 %copy-start = (f32[1024,1024]{1,0:T(8,128)S(1)}, f32[1024,1024]{1,0:T(8,128)}, u32[]{:S(2)}) copy-start(f32[1024,1024]{1,0:T(8,128)} %old_k_ref.3) | copy-start | bytes 12582916
  9.9 31.5 %collective-permute-start.1 = (f32[512,1024]{1,0:T(8,128)}, f32[512,1024]{1,0:T(8,128)S(1)}, u32[]{:S(2)}, u32[]{:S(2)}) collective-permute-start(f32[512,1024]{1,0:T(8,128)} %slice.37), channel_id=1, source_target_pairs={{0,2},{2,4},{4,6},{6,8},{8,10},{10,12},{12,14},{14,16},{16,18},{18... | collective-permute-start | bytes 6291464 | tf_op jit(solution)/shard_map/ppermute | solution.py:17
  15.9 44.3 %collective-permute-start = (f32[512,1024]{1,0:T(8,128)}, f32[512,1024]{1,0:T(8,128)}, u32[]{:S(2)}, u32[]{:S(2)}) collective-permute-start(f32[512,1024]{1,0:T(8,128)} %slice.36), channel_id=1, source_target_pairs={{0,2},{2,4},{4,6},{6,8},{8,10},{10,12},{12,14},{14,16},{16,18},{18... | collective-permute-start | bytes 6291464 | tf_op jit(solution)/shard_map/ppermute | solution.py:17
  17.8 2.2 copy-start.1
  20.0 2.2 copy-start.5
  22.2 2.2 copy-start.9
  24.3 35.8 %copy-start.2 = (f32[1024,1024]{1,0:T(8,128)S(1)}, f32[1024,1024]{1,0:T(8,128)}, u32[]{:S(2)}) copy-start(f32[1024,1024]{1,0:T(8,128)} %old_k_ref.3) | copy-start | bytes 12582916
  24.3 35.8 %copy-start.6 = (f32[1024,1024]{1,0:T(8,128)S(1)}, f32[1024,1024]{1,0:T(8,128)}, u32[]{:S(2)}) copy-start(f32[1024,1024]{1,0:T(8,128)} %old_v_ref.3) | copy-start | bytes 12582916
  79.6 48.8 %all-to-all-start = ((f32[16,2,32,512]{3,2,1,0:T(8,128)}), f32[16,2,32,512]{3,2,1,0:T(8,128)}, u32[]{:S(2)}, u32[]{:S(2)}) async-start(f32[16,2,32,512]{3,2,1,0:T(8,128)} %bitcast.79), calls=%async_computation | async-start | bytes 4194304 | tf_op jit(solution)/shard_map/all_to_all | solution.py:118
  86.8 147.5 %all-gather.3.cloned.1.call-start = ((), (), s32[]{:S(2)}) async-start(), calls=%async_computation.10 | async-start | bytes 6291456 | tf_op jit(solution)/shard_map/all_gather | solution.py:119
  87.0 2.2 copy-start.3
  89.2 2.2 copy-start.7
  91.4 2.2 copy-start.10
  128.4 139.7 %all-gather.5.cloned.1.call-start = ((), (), s32[]{:S(2)}) async-start(), calls=%async_computation.11 | async-start | bytes 6291456 | tf_op jit(solution)/shard_map/all_gather | solution.py:119
  128.4 2.2 copy-start.4
  130.6 2.2 copy-start.8
  132.8 2.2 copy-start.11
  211.6 218.9 %reduce-scatter.11.cloned.1.call-start = ((), (), s32[]{:S(2)}) async-start(), calls=%async_computation.15 | async-start | bytes 3145728 | tf_op jit(solution)/shard_map/reduce_scatter | solution.py:132
  211.7 18.4 %slice-start = ((s8[8388608]{0:T(1024)(128)(4,1)}), s8[4194304]{0:T(1024)(128)(4,1)S(1)}, s32[]{:S(2)}) async-start(s8[8388608]{0:T(1024)(128)(4,1)} %bitcast.75), calls=%async_computation.16 | async-start | bytes 8388608
  220.8 9.3 %slice-start.1 = ((s8[8388608]{0:T(1024)(128)(4,1)}), s8[4194304]{0:T(1024)(128)(4,1)S(1)}, s32[]{:S(2)}) async-start(s8[8388608]{0:T(1024)(128)(4,1)} %bitcast.75), calls=%async_computation.17 | async-start | bytes 8388608
  286.1 2.2 copy-start.17
  286.1 3.5 copy-start.18
  289.6 14.3 %copy-start.13 = (f32[1024,1024]{1,0:T(8,128)S(1)}, f32[1024,1024]{1,0:T(8,128)}, u32[]{:S(2)}) copy-start(f32[1024,1024]{1,0:T(8,128)} %all-gather.5.cloned.1.call-done) | copy-start | bytes 12582916
  289.6 14.3 %copy-start.15 = (f32[2,1,512,1024]{3,2,1,0:T(8,128)S(1)}, f32[2,1,512,1024]{3,2,1,0:T(8,128)}, u32[]{:S(2)}) copy-start(f32[2,1,512,1024]{3,2,1,0:T(8,128)} %get-tuple-element.9) | copy-start | bytes 12582916
  317.9 2.2 copy-start.16
  320.0 15.6 %copy-start.14 = (f32[2,1,512,1024]{3,2,1,0:T(8,128)S(1)}, f32[2,1,512,1024]{3,2,1,0:T(8,128)}, u32[]{:S(2)}) copy-start(f32[2,1,512,1024]{3,2,1,0:T(8,128)} %get-tuple-element.5) | copy-start | bytes 12582916
  387.3 2.0 copy-start.12
  398.5 66.0 %reduce-scatter.9.cloned.1.call-start = ((), (), s32[]{:S(2)}) async-start(), calls=%async_computation.14 | async-start | bytes 3145728 | tf_op jit(solution)/shard_map/reduce_scatter | solution.py:132
  408.8 89.7 %reduce-scatter.7.cloned.1.call-start = ((), (), s32[]{:S(2)}) async-start(), calls=%async_computation.13 | async-start | bytes 3145728 | tf_op jit(solution)/shard_map/reduce_scatter | solution.py:132
  430.5 34.1 %all-to-all-start.5 = ((f32[16,32,512]{2,1,0:T(8,128)}), f32[16,32,512]{2,1,0:T(8,128)S(1)}, u32[]{:S(2)}, u32[]{:S(2)}) async-start(f32[16,32,512]{2,1,0:T(8,128)} %bitcast.93), calls=%async_computation.9 | async-start | bytes 2097152 | tf_op jit(solution)/shard_map/all_to_all | solution.py:134
  436.7 95.9 %reduce-scatter.5.cloned.1.call-start = ((), (), s32[]{:S(2)}) async-start(), calls=%async_computation.12 | async-start | bytes 3145728 | tf_op jit(solution)/shard_map/reduce_scatter | solution.py:132
  464.6 33.9 %all-to-all-start.4 = ((f32[16,32,512]{2,1,0:T(8,128)}), f32[16,32,512]{2,1,0:T(8,128)S(1)}, u32[]{:S(2)}, u32[]{:S(2)}) async-start(f32[16,32,512]{2,1,0:T(8,128)} %bitcast.92), calls=%async_computation.7 | async-start | bytes 2097152 | tf_op jit(solution)/shard_map/all_to_all | solution.py:134
  498.5 34.1 %all-to-all-start.3 = ((f32[16,32,512]{2,1,0:T(8,128)}), f32[16,32,512]{2,1,0:T(8,128)S(1)}, u32[]{:S(2)}, u32[]{:S(2)}) async-start(f32[16,32,512]{2,1,0:T(8,128)} %bitcast.91), calls=%async_computation.5 | async-start | bytes 2097152 | tf_op jit(solution)/shard_map/all_to_all | solution.py:134
Sparse Core Ops, SparseCore 0:
  128.5 62.3 all-gather.2
  211.7 56.2 all-gather.4
  398.6 31.8 reduce-scatter.10
  432.7 31.8 reduce-scatter.8
  466.6 31.8 reduce-scatter.6
  500.7 31.8 reduce-scatter.4

commit v3 on v2

--- a/solution.py
+++ b/solution.py
@@ -87,8 +87,8 @@
     return summed / jnp.transpose(total)[:, :, None]
 
 
-def matmul(left, right):
-    return jnp.dot(left, right, precision=HIGHEST, preferred_element_type=jnp.float32)
+def matmul(left, right, precision=HIGHEST):
+    return jnp.dot(left, right, precision=precision, preferred_element_type=jnp.float32)
 
 
 def local(queries, keys, values, stride_query_w, stride_key_w, stride_value_w, out_weight):
@@ -102,7 +102,7 @@
     not_first = (lax.axis_index("ctx") > 0).astype(jnp.int32).reshape(1, 1)
     old_k = passed_along(keys[rows - BAND :], "ctx", 1)
     old_v = passed_along(values[rows - BAND :], "ctx", 1)
-    groups = 2 if heads_here % 2 == 0 else 1
+    groups = 4 if heads_here % 4 == 0 else 2 if heads_here % 2 == 0 else 1
     part = width // groups
     few = heads_here // groups
     laters = [
@@ -119,7 +119,8 @@
         banded = lax.all_gather(banded.reshape(rows, part), "head", axis=1, tiled=True)
         for at, weight in enumerate(maps):
             met = weight.reshape(across, groups, part, width)[:, group].reshape(-1, width)
-            sums[at] = sums[at] + matmul(banded, met)
+            how = lax.Precision.HIGH if at == 2 else HIGHEST
+            sums[at] = sums[at] + matmul(banded, met, how)
     grouped = (along * (rows // STRIDE), STRIDE // along, heads_here, HSZ)
     q_two, k_two, v_two = (total.reshape(grouped) for total in sums)
     attended = jax.vmap(strided_one, in_axes=2, out_axes=2)(q_two, k_two, v_two)

time: 581 us -> 542 us (0.933)
  blocking collectives: 89.9 us -> 31.4 us
  starting transfers between devices: 32.7 us -> 51.7 us
  waiting for transfers between devices: 137 us -> 129 us
    all_to_all x1 -> x0, blocking collectives: 58.5 us -> none  [local(): lax.all_to_all(banded, 'ctx', split_axis=0, concat_axis=0, tiled=True)]
    all_to_all x1 -> x4, starting transfers between devices: 7.2 us -> 25.3 us  [local(): lax.all_to_all(banded, 'ctx', split_axis=0, concat_axis=0, tiled=True)]
    all_gather x2 -> x4, waiting for transfers between devices: 15.8 us -> 0.01 us  [local(): lax.all_gather(banded.reshape(rows, part), 'head', axis=1, tiled=True)]
    ppermute x2, waiting for transfers between devices: 18.7 us -> 27.2 us  [passed_along(): return lax.ppermute(block, axis, route)]
    unnamed x45 -> x73, local copies, waits for them, and re-layouts: 28.7 us -> 35.8 us
    pallas_call x4 -> x8, Pallas kernels: 69.4 us -> 71.2 us  [band(): pl.pallas_call(band_kernel, grid=(heads, blocks), out_shape=jax.ShapeDtyp...]
    all_to_all x1 -> x4, waiting for transfers between devices: 17.7 us -> 16.4 us  [local(): lax.all_to_all(banded, 'ctx', split_axis=0, concat_axis=0, tiled=True)]
    dot_general x10 -> x16, matrix products: 134 us -> 134 us  [matmul(): jnp.dot(left, right, precision=precision, preferred_element_type=jnp.floa...]
  transfers between devices with their start and end apart: 12 -> 17, of which waited for: 7 -> 7; matrix products, arithmetic and copies ran while one was open for 13% -> 16% of each run, Pallas kernels for 9% -> 12%
where the time goes in v3:
time: 542 us; the launch traced here: 534 us
  matrix products  157 us (29%)
  waiting for transfers between devices  129 us (24%)
  local copies, waits for them, and re-layouts  74.8 us (14%)
  Pallas kernels  71.2 us (13%)
  starting transfers between devices  51.7 us (10%)
  blocking collectives  31.4 us (6%)
  between operations  14.5 us (3%)
    dot_general x16, matrix products, matmul(): jnp.dot(left, right, precision=precision, preferred_element_type=jnp.floa...  134 us
    reduce_scatter x4, waiting for transfers between devices, local(): mixed = lax.psum_scatter(share, 'head', scatter_dimension=0, tiled=True)  85.7 us
    pallas_call x8, Pallas kernels, band(): pl.pallas_call(band_kernel, grid=(heads, blocks), out_shape=jax.ShapeDtyp...  71.2 us
    unnamed x73, local copies, waits for them, and re-layouts  35.8 us
    all_to_all x1, blocking collectives, local(): lax.all_to_all(mixed, 'ctx', split_axis=0, concat_axis=0, tiled=True)  31.4 us
    ppermute x2, waiting for transfers between devices, passed_along(): return lax.ppermute(block, axis, route)  27.2 us
    all_to_all x4, starting transfers between devices, local(): lax.all_to_all(banded, 'ctx', split_axis=0, concat_axis=0, tiled=True)  25.3 us
    all_to_all x3, starting transfers between devices, local(): lax.all_to_all(mixed, 'ctx', split_axis=0, concat_axis=0, tiled=True)  18.6 us
  transfers between devices with their start and end apart: 17, of which 7 were waited for; matrix products, arithmetic and copies ran while one was open for 16% of the time, Pallas kernels for 12%

profile of v3, /device:TPU:1, one launch (start us, length us, event | category | flops | bytes accessed | tf_op | source)
XLA Modules:
  0.0 534.2 jit_solution(3595670964442785658)
XLA Ops:
  6.5 3.3 slice.54
  9.8 4.5 collective-permute-start
  24.4 8.5 %shard_map.74 = f32[512,256]{1,0:T(8,128)S(1)} custom-call(s32[1,1]{1,0:T(1,128)} %constant.5.clone.1.valid_ref, f32[1024,1024]{1,0:T(8,128)S(1)} %copy-done.17, f32[1024,1024]{1,0:T(8,128)S(1)} %copy-done, f32[1024,1024]{1,0:T(8,128)S(1)} %copy-done.9, f32[1024,1024]{1,0:T(8,128)S(1)} %copy-done, f32[1024,1024]{1,0:T(8,128)S(1)} %copy-done.9), custom_call_target="tpu_custom_call" | custom-call | flops 2415919104 | bytes 3145728 | tf_op jit(solution)/shard_map/pallas_call | solution.py:56
  32.9 4.7 collective-permute-done.old_k_ref
  37.6 22.5 %collective-permute-done.1.old_v_ref = f32[512,1024]{1,0:T(8,128)} collective-permute-done((f32[512,1024]{1,0:T(8,128)}, f32[512,1024]{1,0:T(8,128)}, u32[]{:S(2)}, u32[]{:S(2)}) %collective-permute-start.1) | collective-permute-done | bytes 2097184 | tf_op jit(solution)/shard_map/ppermute | solution.py:17
  60.1 9.2 %shard_map.73 = f32[512,256]{1,0:T(8,128)S(1)} custom-call(s32[1,1]{1,0:T(1,128)} %bitcast.valid_ref, f32[1024,1024]{1,0:T(8,128)S(1)} %copy-done.17, f32[1024,1024]{1,0:T(8,128)S(1)} %copy-done.1, f32[1024,1024]{1,0:T(8,128)S(1)} %copy-done.10, f32[512,1024]{1,0:T(8,128)S(1)} %collective-permute-done.old_k_ref, f32[512,1024]{1,0:T(8,128)} %collective-permute-done.1.old_v_ref), custom_call_target="tpu_custom_call" | custom-call | flops 2415919104 | bytes 3145728 | tf_op jit(solution)/shard_map/pallas_call | solution.py:56
  70.5 7.2 %all-to-all-start = ((f32[16,2,32,256]{3,2,1,0:T(8,128)}), f32[16,2,32,256]{3,2,1,0:T(8,128)}, u32[]{:S(2)}, u32[]{:S(2)}) async-start(f32[16,2,32,256]{3,2,1,0:T(8,128)} %bitcast.90), calls=%async_computation | async-start | bytes 2097152 | tf_op jit(solution)/shard_map/all_to_all | solution.py:118
  84.5 8.5 %shard_map.76 = f32[512,256]{1,0:T(8,128)S(1)} custom-call(s32[1,1]{1,0:T(1,128)} %constant.5.clone.1.valid_ref, f32[1024,1024]{1,0:T(8,128)S(1)} %copy-done.18, f32[1024,1024]{1,0:T(8,128)S(1)} %copy-done.2, f32[1024,1024]{1,0:T(8,128)S(1)} %copy-done.11, f32[1024,1024]{1,0:T(8,128)S(1)} %copy-done.2, f32[1024,1024]{1,0:T(8,128)S(1)} %copy-done.11), custom_call_target="tpu_custom_call" | custom-call | flops 2415919104 | bytes 3145728 | tf_op jit(solution)/shard_map/pallas_call | solution.py:56
  93.1 9.3 %shard_map.75 = f32[512,256]{1,0:T(8,128)S(1)} custom-call(s32[1,1]{1,0:T(1,128)} %bitcast.valid_ref, f32[1024,1024]{1,0:T(8,128)S(1)} %copy-done.18, f32[1024,1024]{1,0:T(8,128)S(1)} %copy-done.3, f32[1024,1024]{1,0:T(8,128)S(1)} %copy-done.12, f32[512,1024]{1,0:T(8,128)S(1)} %collective-permute-done.old_k_ref, f32[512,1024]{1,0:T(8,128)} %collective-permute-done.1.old_v_ref), custom_call_target="tpu_custom_call" | custom-call | flops 2415919104 | bytes 3145728 | tf_op jit(solution)/shard_map/pallas_call | solution.py:56
  103.5 6.0 %all-to-all-start.1 = ((f32[16,2,32,256]{3,2,1,0:T(8,128)}), f32[16,2,32,256]{3,2,1,0:T(8,128)}, u32[]{:S(2)}, u32[]{:S(2)}) async-start(f32[16,2,32,256]{3,2,1,0:T(8,128)} %bitcast.89), calls=%async_computation.1 | async-start | bytes 2097152 | tf_op jit(solution)/shard_map/all_to_all | solution.py:118
  117.1 8.5 %shard_map.78 = f32[512,256]{1,0:T(8,128)S(1)} custom-call(s32[1,1]{1,0:T(1,128)} %constant.5.clone.1.valid_ref, f32[1024,1024]{1,0:T(8,128)S(1)} %copy-done.19, f32[1024,1024]{1,0:T(8,128)S(1)} %copy-done.4, f32[1024,1024]{1,0:T(8,128)S(1)} %copy-done.13, f32[1024,1024]{1,0:T(8,128)S(1)} %copy-done.4, f32[1024,1024]{1,0:T(8,128)S(1)} %copy-done.13), custom_call_target="tpu_custom_call" | custom-call | flops 2415919104 | bytes 3145728 | tf_op jit(solution)/shard_map/pallas_call | solution.py:56
  125.6 9.3 %shard_map.77 = f32[512,256]{1,0:T(8,128)S(1)} custom-call(s32[1,1]{1,0:T(1,128)} %bitcast.valid_ref, f32[1024,1024]{1,0:T(8,128)S(1)} %copy-done.19, f32[1024,1024]{1,0:T(8,128)S(1)} %copy-done.5, f32[1024,1024]{1,0:T(8,128)S(1)} %copy-done.14, f32[512,1024]{1,0:T(8,128)S(1)} %collective-permute-done.old_k_ref, f32[512,1024]{1,0:T(8,128)} %collective-permute-done.1.old_v_ref), custom_call_target="tpu_custom_call" | custom-call | flops 2415919104 | bytes 3145728 | tf_op jit(solution)/shard_map/pallas_call | solution.py:56
  136.1 6.0 %all-to-all-start.2 = ((f32[16,2,32,256]{3,2,1,0:T(8,128)}), f32[16,2,32,256]{3,2,1,0:T(8,128)}, u32[]{:S(2)}, u32[]{:S(2)}) async-start(f32[16,2,32,256]{3,2,1,0:T(8,128)} %bitcast.88), calls=%async_computation.2 | async-start | bytes 2097152 | tf_op jit(solution)/shard_map/all_to_all | solution.py:118
  149.8 8.5 %shard_map.80 = f32[512,256]{1,0:T(8,128)S(1)} custom-call(s32[1,1]{1,0:T(1,128)} %constant.5.clone.1.valid_ref, f32[1024,1024]{1,0:T(8,128)S(1)} %copy-done.20, f32[1024,1024]{1,0:T(8,128)S(1)} %copy-done.6, f32[1024,1024]{1,0:T(8,128)S(1)} %copy-done.15, f32[1024,1024]{1,0:T(8,128)S(1)} %copy-done.6, f32[1024,1024]{1,0:T(8,128)S(1)} %copy-done.15), custom_call_target="tpu_custom_call" | custom-call | flops 2415919104 | bytes 3145728 | tf_op jit(solution)/shard_map/pallas_call | solution.py:56
  158.4 9.3 %shard_map.79 = f32[512,256]{1,0:T(8,128)S(1)} custom-call(s32[1,1]{1,0:T(1,128)} %bitcast.valid_ref, f32[1024,1024]{1,0:T(8,128)S(1)} %copy-done.20, f32[1024,1024]{1,0:T(8,128)S(1)} %copy-done.7, f32[1024,1024]{1,0:T(8,128)S(1)} %copy-done.16, f32[512,1024]{1,0:T(8,128)S(1)} %collective-permute-done.old_k_ref, f32[512,1024]{1,0:T(8,128)} %collective-permute-done.1.old_v_ref), custom_call_target="tpu_custom_call" | custom-call | flops 2415919104 | bytes 3145728 | tf_op jit(solution)/shard_map/pallas_call | solution.py:56
  168.9 6.0 %all-to-all-start.3 = ((f32[16,2,32,256]{3,2,1,0:T(8,128)}), f32[16,2,32,256]{3,2,1,0:T(8,128)S(1)}, u32[]{:S(2)}, u32[]{:S(2)}) async-start(f32[16,2,32,256]{3,2,1,0:T(8,128)} %bitcast.87), calls=%async_computation.3 | async-start | bytes 2097152 | tf_op jit(solution)/shard_map/all_to_all | solution.py:118
  175.0 6.7 %fusion.24 = (f32[2,1,256,1024]{3,2,1,0:T(8,128)S(1)}, f32[2,1,256,1024]{3,2,1,0:T(8,128)}, f32[2,1,256,1024]{3,2,1,0:T(8,128)}, f32[2,1,256,1024]{3,2,1,0:T(8,128)}) fusion(f32[2,4,256,1024]{3,2,1,0:T(8,128)} %bitcast.98), kind=kLoop, calls=%fused_computation.38 | loop fusion | bytes 16777216 | tf_op jit(solution)/shard_map/slice | solution.py:121
  181.7 16.4 %all-to-all-done.3 = f32[16,2,32,256]{3,2,1,0:T(8,128)S(1)} async-done(((f32[16,2,32,256]{3,2,1,0:T(8,128)}), f32[16,2,32,256]{3,2,1,0:T(8,128)S(1)}, u32[]{:S(2)}, u32[]{:S(2)}) %all-to-all-start.3) | async-done | bytes 1048608 | tf_op jit(solution)/shard_map/all_to_all | solution.py:118
  199.3 7.8 %fusion.25 = (f32[2,1,256,1024]{3,2,1,0:T(8,128)}, f32[2,1,256,1024]{3,2,1,0:T(8,128)}, f32[2,1,256,1024]{3,2,1,0:T(8,128)}, f32[2,1,256,1024]{3,2,1,0:T(8,128)}) fusion(f32[2,4,256,1024]{3,2,1,0:T(8,128)} %bitcast.99), kind=kLoop, calls=%fused_computation.39 | loop fusion | bytes 16777216 | tf_op jit(solution)/shard_map/slice | solution.py:121
  207.5 3.6 fusion.23
  211.1 10.2 %fusion.29 = f32[1024,1024]{1,0:T(8,128)} fusion(f32[1024,512]{1,0:T(8,128)} %all-gather.5.cloned.1.call-done, f32[512,1024]{1,0:T(8,128)} %bitcast.114), kind=kOutput, calls=%fused_computation.43 | convolution fusion | flops 6442450944 | bytes 8388608 | tf_op jit(solution)/shard_map/dot_general | solution.py:91
  221.3 10.2 %fusion.30 = f32[1024,1024]{1,0:T(8,128)} fusion(f32[1024,512]{1,0:T(8,128)} %all-gather.7.cloned.1.call-done, f32[512,1024]{1,0:T(8,128)} %bitcast.113), kind=kOutput, calls=%fused_computation.44 | convolution fusion | flops 6442450944 | bytes 8388608 | tf_op jit(solution)/shard_map/dot_general | solution.py:91
  231.6 10.1 %fusion.31 = f32[1024,1024]{1,0:T(8,128)} fusion(f32[1024,512]{1,0:T(8,128)} %all-gather.9.cloned.1.call-done, f32[512,1024]{1,0:T(8,128)} %bitcast.109), kind=kOutput, calls=%fused_computation.45 | convolution fusion | flops 6442450944 | bytes 8388608 | tf_op jit(solution)/shard_map/dot_general | solution.py:91
  241.7 13.5 %add_bitcast_fusion.1 = f32[128,8,8,128]{3,1,2,0:T(8,128)S(1)} fusion(f32[1024,1024]{1,0:T(8,128)} %fusion.31, f32[1024,1024]{1,0:T(8,128)} %fusion.29, f32[1024,1024]{1,0:T(8,128)} %fusion.30, f32[1024,512]{1,0:T(8,128)} %all-gather.11.cloned.1.call-done, f32[512,1024]{1,0:T(8,128)S(1)} %bitcast.104), kind=kOutput, calls=%fused_computation.10 | convolution fusion | flops 6445596672 | bytes 20971520 | tf_op jit(solution)/shard_map/dot_general | solution.py:91
  257.4 7.3 %fusion.32 = f32[1024,1024]{1,0:T(8,128)S(1)} fusion(f32[1024,512]{1,0:T(8,128)S(1)} %copy-done.23, f32[512,1024]{1,0:T(8,128)S(1)} %bitcast.112), kind=kOutput, calls=%fused_computation.46 | convolution fusion | flops 6442450944 | bytes 8388608 | tf_op jit(solution)/shard_map/dot_general | solution.py:91
  264.8 7.5 %fusion.33 = f32[1024,1024]{1,0:T(8,128)S(1)} fusion(f32[1024,512]{1,0:T(8,128)S(1)} %copy-done.24, f32[512,1024]{1,0:T(8,128)S(1)} %bitcast.111), kind=kOutput, calls=%fused_computation.47 | convolution fusion | flops 6442450944 | bytes 8388608 | tf_op jit(solution)/shard_map/dot_general | solution.py:91
  272.3 7.3 %fusion.34 = f32[1024,1024]{1,0:T(8,128)S(1)} fusion(f32[1024,512]{1,0:T(8,128)S(1)} %copy-done.25, f32[512,1024]{1,0:T(8,128)S(1)} %bitcast.110), kind=kOutput, calls=%fused_computation.48 | convolution fusion | flops 6442450944 | bytes 8388608 | tf_op jit(solution)/shard_map/dot_general | solution.py:91
  279.7 9.8 %add_bitcast_fusion = f32[128,8,8,128]{3,1,2,0:T(8,128)S(1)} fusion(f32[1024,1024]{1,0:T(8,128)S(1)} %fusion.34, f32[1024,1024]{1,0:T(8,128)S(1)} %fusion.32, f32[1024,1024]{1,0:T(8,128)S(1)} %fusion.33, f32[1024,512]{1,0:T(8,128)S(1)} %copy-done.22, f32[512,1024]{1,0:T(8,128)} %bitcast.105), kind=kOutput, calls=%fused_computation.9 | convolution fusion | flops 6445596672 | bytes 20971520 | tf_op jit(solution)/shard_map/dot_general | solution.py:91
  291.1 3.6 fusion.26
  294.8 3.6 fusion.27
  298.4 4.1 fusion.28
  302.5 5.9 %add_bitcast_fusion.2 = f32[128,8,8,128]{3,1,2,0:T(8,128)S(1)} fusion(f32[1024,1024]{1,0:T(8,128)S(1)} %fusion.28, f32[1024,1024]{1,0:T(8,128)S(1)} %fusion.26, f32[1024,1024]{1,0:T(8,128)S(1)} %fusion.27, f32[1024,512]{1,0:T(8,128)S(1)} %copy-done.22, f32[512,1024]{1,0:T(8,128)} %bitcast.103), kind=kOutput, calls=%fused_computation.11 | convolution fusion | flops 3224371200 | bytes 20971520 | tf_op jit(solution)/shard_map/dot_general | solution.py:91
  309.5 11.9 %fusion.5 = (f32[8,32,32]{2,1,0:T(8,128)S(1)}, f32[8,32,32,32]{2,3,1,0:T(8,128)S(1)}) fusion(pred[32,32]{0,1:T(8,128)(4,1)S(1)} %iota_compare_fusion, f32[32,32,8,128]{3,2,1,0:T(8,128)S(1)} %bitcast.96, f32[32,32,8,128]{3,2,1,0:T(8,128)S(1)} %bitcast.95), kind=kOutput, calls=%fused_computation.12 | convolution fusion | flops 403431424 | bytes 9470976 | tf_op jit(solution)/shard_map/vmap(brd,crd->rbc)/dot_general | solution.py:77
  322.9 11.0 %bitcast_divide_fusion = f32[32,32,8,128]{3,0,1,2:T(8,128)S(1)} fusion(f32[32,32,8]{0,1,2:T(8,128)S(1)} %bitcast.129, f32[8,32,32,32]{2,3,1,0:T(8,128)S(1)} %get-tuple-element.18, f32[8,32,32]{2,1,0:T(8,128)S(1)} %get-tuple-element.17, pred[32,32]{0,1:T(8,128)(4,1)S(1)} %iota_compare_fusion, f32[32,32,8,128]{3,2,1,0:T(8,128)S(1)} %bitcast.115), kind=kOutput, calls=%fused_computation.1 | convolution fusion | flops 404488192 | bytes 9503744 | tf_op jit(solution)/shard_map/vmap(rbc,crd->brd)/dot_general | solution.py:86
  333.9 4.4 copy.20
  338.3 4.9 reshape.104
  347.8 9.4 %fusion.13 = f32[1024,512]{1,0:T(8,128)} fusion(f32[1024,1024]{1,0:T(8,128)S(1)} %bitcast.91, f32[1024,2048]{1,0:T(8,128)} %param.13), kind=kOutput, calls=%fused_computation.20 | convolution fusion | flops 6442450944 | bytes 8388608 | tf_op jit(solution)/shard_map/dot_general | solution.py:91
  357.3 10.2 %fusion.11 = f32[1024,512]{1,0:T(8,128)} fusion(f32[1024,1024]{1,0:T(8,128)} %bitcast.92, f32[1024,2048]{1,0:T(8,128)} %param.13), kind=kOutput, calls=%fused_computation.18 | convolution fusion | flops 6442450944 | bytes 8388608 | tf_op jit(solution)/shard_map/dot_general | solution.py:91
  367.6 10.2 %fusion.9 = f32[1024,512]{1,0:T(8,128)} fusion(f32[1024,1024]{1,0:T(8,128)} %bitcast.93, f32[1024,2048]{1,0:T(8,128)} %param.13), kind=kOutput, calls=%fused_computation.16 | convolution fusion | flops 6442450944 | bytes 8388608 | tf_op jit(solution)/shard_map/dot_general | solution.py:91
  377.8 12.8 %reduce-scatter.5.cloned.1.call-done = f32[512,512]{1,0:T(8,128)} async-done(((f32[1024,512]{1,0:T(8,128)}), f32[512,512]{1,0:T(8,128)}) %reduce-scatter.5.cloned.1.call-update) | async-done | bytes 1048592 | tf_op jit(solution)/shard_map/reduce_scatter | solution.py:133
  390.6 6.2 %all-to-all-start.4 = ((f32[16,32,512]{2,1,0:T(8,128)}), f32[16,32,512]{2,1,0:T(8,128)S(1)}, u32[]{:S(2)}, u32[]{:S(2)}) async-start(f32[16,32,512]{2,1,0:T(8,128)} %bitcast.127), calls=%async_computation.5 | async-start | bytes 2097152 | tf_op jit(solution)/shard_map/all_to_all | solution.py:135
  396.9 10.7 %fusion.7 = f32[1024,512]{1,0:T(8,128)} fusion(f32[1024,1024]{1,0:T(8,128)} %bitcast.94, f32[1024,2048]{1,0:T(8,128)} %param.13), kind=kOutput, calls=%fused_computation.14 | convolution fusion | flops 6442450944 | bytes 8388608 | tf_op jit(solution)/shard_map/dot_general | solution.py:91
  407.6 17.1 %reduce-scatter.7.cloned.1.call-done = f32[512,512]{1,0:T(8,128)} async-done(((f32[1024,512]{1,0:T(8,128)}), f32[512,512]{1,0:T(8,128)}) %reduce-scatter.7.cloned.1.call-update) | async-done | bytes 1048592 | tf_op jit(solution)/shard_map/reduce_scatter | solution.py:133
  424.7 6.2 %all-to-all-start.5 = ((f32[16,32,512]{2,1,0:T(8,128)}), f32[16,32,512]{2,1,0:T(8,128)S(1)}, u32[]{:S(2)}, u32[]{:S(2)}) async-start(f32[16,32,512]{2,1,0:T(8,128)} %bitcast.126), calls=%async_computation.7 | async-start | bytes 2097152 | tf_op jit(solution)/shard_map/all_to_all | solution.py:135
  430.9 27.9 %reduce-scatter.9.cloned.1.call-done = f32[512,512]{1,0:T(8,128)} async-done(((f32[1024,512]{1,0:T(8,128)}), f32[512,512]{1,0:T(8,128)}) %reduce-scatter.9.cloned.1.call-update) | async-done | bytes 1048592 | tf_op jit(solution)/shard_map/reduce_scatter | solution.py:133
  458.8 6.2 %all-to-all-start.6 = ((f32[16,32,512]{2,1,0:T(8,128)}), f32[16,32,512]{2,1,0:T(8,128)S(1)}, u32[]{:S(2)}, u32[]{:S(2)}) async-start(f32[16,32,512]{2,1,0:T(8,128)} %bitcast.125), calls=%async_computation.9 | async-start | bytes 2097152 | tf_op jit(solution)/shard_map/all_to_all | solution.py:135
  465.0 28.0 %reduce-scatter.11.cloned.1.call-done = f32[512,512]{1,0:T(8,128)} async-done(((f32[1024,512]{1,0:T(8,128)}), f32[512,512]{1,0:T(8,128)}) %reduce-scatter.11.cloned.1.call-update) | async-done | bytes 1048592 | tf_op jit(solution)/shard_map/reduce_scatter | solution.py:133
  493.0 31.4 %all_to_all.40 = f32[16,32,512]{2,1,0:T(8,128)S(1)} all-to-all(f32[16,32,512]{2,1,0:T(8,128)} %bitcast.128), channel_id=1, replica_groups=mesh['ctx'=16,'head'=2] {'ctx'}, dimensions={0} | all-to-all | bytes 2097152 | tf_op jit(solution)/shard_map/all_to_all | solution.py:135
  (114 shorter events, 51.7 us)
Async XLA Ops:
  6.5 7.8 %copy-start.8 = (f32[1024,1024]{1,0:T(8,128)S(1)}, f32[1024,1024]{1,0:T(8,128)}, u32[]{:S(2)}) copy-start(f32[1024,1024]{1,0:T(8,128)} %old_v_ref.7) | copy-start | bytes 12582916
  9.8 27.8 %collective-permute-start = (f32[512,1024]{1,0:T(8,128)}, f32[512,1024]{1,0:T(8,128)S(1)}, u32[]{:S(2)}, u32[]{:S(2)}) collective-permute-start(f32[512,1024]{1,0:T(8,128)} %slice.54), channel_id=1, source_target_pairs={{0,2},{2,4},{4,6},{6,8},{8,10},{10,12},{12,14},{14,16},{16,18},{18... | collective-permute-start | bytes 6291464 | tf_op jit(solution)/shard_map/ppermute | solution.py:17
  15.9 44.2 %collective-permute-start.1 = (f32[512,1024]{1,0:T(8,128)}, f32[512,1024]{1,0:T(8,128)}, u32[]{:S(2)}, u32[]{:S(2)}) collective-permute-start(f32[512,1024]{1,0:T(8,128)} %slice.55), channel_id=1, source_target_pairs={{0,2},{2,4},{4,6},{6,8},{8,10},{10,12},{12,14},{14,16},{16,18},{18... | collective-permute-start | bytes 6291464 | tf_op jit(solution)/shard_map/ppermute | solution.py:17
  17.8 2.2 copy-start
  20.0 2.2 copy-start.9
  22.2 2.2 copy-start.17
  24.4 35.7 %copy-start.1 = (f32[1024,1024]{1,0:T(8,128)S(1)}, f32[1024,1024]{1,0:T(8,128)}, u32[]{:S(2)}) copy-start(f32[1024,1024]{1,0:T(8,128)} %old_k_ref.7) | copy-start | bytes 12582916
  24.4 35.7 %copy-start.10 = (f32[1024,1024]{1,0:T(8,128)S(1)}, f32[1024,1024]{1,0:T(8,128)}, u32[]{:S(2)}) copy-start(f32[1024,1024]{1,0:T(8,128)} %old_v_ref.7) | copy-start | bytes 12582916
  70.5 31.9 %all-to-all-start = ((f32[16,2,32,256]{3,2,1,0:T(8,128)}), f32[16,2,32,256]{3,2,1,0:T(8,128)}, u32[]{:S(2)}, u32[]{:S(2)}) async-start(f32[16,2,32,256]{3,2,1,0:T(8,128)} %bitcast.90), calls=%async_computation | async-start | bytes 2097152 | tf_op jit(solution)/shard_map/all_to_all | solution.py:118
  77.7 133.4 %all-gather.5.cloned.1.call-start = ((), (), s32[]{:S(2)}) async-start(), calls=%async_computation.12 | async-start | bytes 3145728 | tf_op jit(solution)/shard_map/all_gather | solution.py:119
  78.0 2.2 copy-start.2
  80.2 2.2 copy-start.11
  82.3 2.2 copy-start.18
  84.5 8.6 %copy-start.3 = (f32[1024,1024]{1,0:T(8,128)S(1)}, f32[1024,1024]{1,0:T(8,128)}, u32[]{:S(2)}) copy-start(f32[1024,1024]{1,0:T(8,128)} %old_k_ref.7) | copy-start | bytes 12582916
  84.5 8.6 %copy-start.12 = (f32[1024,1024]{1,0:T(8,128)S(1)}, f32[1024,1024]{1,0:T(8,128)}, u32[]{:S(2)}) copy-start(f32[1024,1024]{1,0:T(8,128)} %old_v_ref.7) | copy-start | bytes 12582916
  103.5 31.4 %all-to-all-start.1 = ((f32[16,2,32,256]{3,2,1,0:T(8,128)}), f32[16,2,32,256]{3,2,1,0:T(8,128)}, u32[]{:S(2)}, u32[]{:S(2)}) async-start(f32[16,2,32,256]{3,2,1,0:T(8,128)} %bitcast.89), calls=%async_computation.1 | async-start | bytes 2097152 | tf_op jit(solution)/shard_map/all_to_all | solution.py:118
  109.6 111.8 %all-gather.7.cloned.1.call-start = ((), (), s32[]{:S(2)}) async-start(), calls=%async_computation.13 | async-start | bytes 3145728 | tf_op jit(solution)/shard_map/all_gather | solution.py:119
  109.9 2.6 copy-start.4
  112.5 2.4 copy-start.13
  114.9 2.2 copy-start.19
  117.1 8.6 %copy-start.5 = (f32[1024,1024]{1,0:T(8,128)S(1)}, f32[1024,1024]{1,0:T(8,128)}, u32[]{:S(2)}) copy-start(f32[1024,1024]{1,0:T(8,128)} %old_k_ref.7) | copy-start | bytes 12582916
  117.1 8.6 %copy-start.14 = (f32[1024,1024]{1,0:T(8,128)S(1)}, f32[1024,1024]{1,0:T(8,128)}, u32[]{:S(2)}) copy-start(f32[1024,1024]{1,0:T(8,128)} %old_v_ref.7) | copy-start | bytes 12582916
  136.1 31.6 %all-to-all-start.2 = ((f32[16,2,32,256]{3,2,1,0:T(8,128)}), f32[16,2,32,256]{3,2,1,0:T(8,128)}, u32[]{:S(2)}, u32[]{:S(2)}) async-start(f32[16,2,32,256]{3,2,1,0:T(8,128)} %bitcast.88), calls=%async_computation.2 | async-start | bytes 2097152 | tf_op jit(solution)/shard_map/all_to_all | solution.py:118
  142.1 89.5 %all-gather.9.cloned.1.call-start = ((), (), s32[]{:S(2)}) async-start(), calls=%async_computation.14 | async-start | bytes 3145728 | tf_op jit(solution)/shard_map/all_gather | solution.py:119
  142.6 2.4 copy-start.6
  145.0 2.5 copy-start.15
  147.5 2.3 copy-start.20
  149.8 8.6 %copy-start.7 = (f32[1024,1024]{1,0:T(8,128)S(1)}, f32[1024,1024]{1,0:T(8,128)}, u32[]{:S(2)}) copy-start(f32[1024,1024]{1,0:T(8,128)} %old_k_ref.7) | copy-start | bytes 12582916
  149.8 8.6 %copy-start.16 = (f32[1024,1024]{1,0:T(8,128)S(1)}, f32[1024,1024]{1,0:T(8,128)}, u32[]{:S(2)}) copy-start(f32[1024,1024]{1,0:T(8,128)} %old_v_ref.7) | copy-start | bytes 12582916
  168.9 29.2 %all-to-all-start.3 = ((f32[16,2,32,256]{3,2,1,0:T(8,128)}), f32[16,2,32,256]{3,2,1,0:T(8,128)S(1)}, u32[]{:S(2)}, u32[]{:S(2)}) async-start(f32[16,2,32,256]{3,2,1,0:T(8,128)} %bitcast.87), calls=%async_computation.3 | async-start | bytes 2097152 | tf_op jit(solution)/shard_map/all_to_all | solution.py:118
  174.9 66.8 %all-gather.11.cloned.1.call-start = ((), (), s32[]{:S(2)}) async-start(), calls=%async_computation.15 | async-start | bytes 3145728 | tf_op jit(solution)/shard_map/all_gather | solution.py:119
  199.1 191.6 %reduce-scatter.5.cloned.1.call-start = ((), (), s32[]{:S(2)}) async-start(), calls=%async_computation.16 | async-start | bytes 3145728 | tf_op jit(solution)/shard_map/reduce_scatter | solution.py:133
  199.3 7.8 %slice-start = ((s8[8388608]{0:T(1024)(128)(4,1)}), s8[4194304]{0:T(1024)(128)(4,1)S(1)}, s32[]{:S(2)}) async-start(s8[8388608]{0:T(1024)(128)(4,1)} %bitcast.100), calls=%async_computation.20 | async-start | bytes 8388608
  199.3 8.2 %slice-start.1 = ((s8[8388608]{0:T(1024)(128)(4,1)}), s8[4194304]{0:T(1024)(128)(4,1)S(1)}, s32[]{:S(2)}) async-start(s8[8388608]{0:T(1024)(128)(4,1)} %bitcast.100), calls=%async_computation.21 | async-start | bytes 8388608
  255.2 2.2 copy-start.31
  257.4 7.3 %copy-start.24 = (f32[1024,512]{1,0:T(8,128)S(1)}, f32[1024,512]{1,0:T(8,128)}, u32[]{:S(2)}) copy-start(f32[1024,512]{1,0:T(8,128)} %all-gather.7.cloned.1.call-done) | copy-start | bytes 6291460
  257.4 7.3 %copy-start.30 = (f32[2,1,256,1024]{3,2,1,0:T(8,128)S(1)}, f32[2,1,256,1024]{3,2,1,0:T(8,128)}, u32[]{:S(2)}) copy-start(f32[2,1,256,1024]{3,2,1,0:T(8,128)} %get-tuple-element.15) | copy-start | bytes 6291460
  264.8 7.5 %copy-start.25 = (f32[1024,512]{1,0:T(8,128)S(1)}, f32[1024,512]{1,0:T(8,128)}, u32[]{:S(2)}) copy-start(f32[1024,512]{1,0:T(8,128)} %all-gather.9.cloned.1.call-done) | copy-start | bytes 6291460
  264.8 7.5 %copy-start.29 = (f32[2,1,256,1024]{3,2,1,0:T(8,128)S(1)}, f32[2,1,256,1024]{3,2,1,0:T(8,128)}, u32[]{:S(2)}) copy-start(f32[2,1,256,1024]{3,2,1,0:T(8,128)} %get-tuple-element.14) | copy-start | bytes 6291460
  272.3 7.3 %copy-start.22 = (f32[1024,512]{1,0:T(8,128)S(1)}, f32[1024,512]{1,0:T(8,128)}, u32[]{:S(2)}) copy-start(f32[1024,512]{1,0:T(8,128)} %all-gather.11.cloned.1.call-done) | copy-start | bytes 6291460
  291.1 3.6 copy-start.27
  294.8 3.7 copy-start.26
  357.2 67.5 %reduce-scatter.7.cloned.1.call-start = ((), (), s32[]{:S(2)}) async-start(), calls=%async_computation.17 | async-start | bytes 3145728 | tf_op jit(solution)/shard_map/reduce_scatter | solution.py:133
  367.5 91.3 %reduce-scatter.9.cloned.1.call-start = ((), (), s32[]{:S(2)}) async-start(), calls=%async_computation.18 | async-start | bytes 3145728 | tf_op jit(solution)/shard_map/reduce_scatter | solution.py:133
  390.6 34.1 %all-to-all-start.4 = ((f32[16,32,512]{2,1,0:T(8,128)}), f32[16,32,512]{2,1,0:T(8,128)S(1)}, u32[]{:S(2)}, u32[]{:S(2)}) async-start(f32[16,32,512]{2,1,0:T(8,128)} %bitcast.127), calls=%async_computation.5 | async-start | bytes 2097152 | tf_op jit(solution)/shard_map/all_to_all | solution.py:135
  396.9 96.1 %reduce-scatter.11.cloned.1.call-start = ((), (), s32[]{:S(2)}) async-start(), calls=%async_computation.19 | async-start | bytes 3145728 | tf_op jit(solution)/shard_map/reduce_scatter | solution.py:133
  424.7 34.1 %all-to-all-start.5 = ((f32[16,32,512]{2,1,0:T(8,128)}), f32[16,32,512]{2,1,0:T(8,128)S(1)}, u32[]{:S(2)}, u32[]{:S(2)}) async-start(f32[16,32,512]{2,1,0:T(8,128)} %bitcast.126), calls=%async_computation.7 | async-start | bytes 2097152 | tf_op jit(solution)/shard_map/all_to_all | solution.py:135
  458.8 34.2 %all-to-all-start.6 = ((f32[16,32,512]{2,1,0:T(8,128)}), f32[16,32,512]{2,1,0:T(8,128)S(1)}, u32[]{:S(2)}, u32[]{:S(2)}) async-start(f32[16,32,512]{2,1,0:T(8,128)} %bitcast.125), calls=%async_computation.9 | async-start | bytes 2097152 | tf_op jit(solution)/shard_map/all_to_all | solution.py:135
  (4 other events, 6.2 us)
Sparse Core Ops, SparseCore 0:
  102.5 33.8 all-gather.4
  138.0 33.1 all-gather.6
  172.7 33.1 all-gather.8
  207.3 33.1 all-gather.10
  357.3 33.2 reduce-scatter.4
  392.8 31.8 reduce-scatter.6
  426.9 31.8 reduce-scatter.8
  461.2 31.8 reduce-scatter.10
